TPU v7x, 256 devices: a whole 4x4x8 slice. The times are simulated.
256 devices in a mesh: gx: 32 (over x, z), gz: 8 (over y, core).
Axes of the slice: x: 4, y: 4, z: 8, core: 2. Of those that a mesh axis runs over, the one named last changes fastest.
Arguments:
- potential: float32 [32, 2048, 2048], P('gz', 'gx'), may hold values from -6 to 6
- regions: int32 [32, 2048, 2048], P('gz', 'gx'), may hold values from 0 to 15, as said below
- charge: float32 [32, 2048, 2048], P('gz', 'gx'), may hold values from -6 to 6
- levels: float32 [16], replicated, may hold values from -2 to 2
Outputs:
- field_out: float32 [32, 2048, 2048], P('gz', 'gx')
- multipoles: float32 [32, 64], P('gz', 'gx')
Inputs may be any that keep to these rules, and one draw needn't show every extreme that they name: `regions`: about three quarters of the cells are free space (id 0); the others carry ids 1 to 15 evenly.
All inputs are finite; a program needn't handle non-finite values.
Results may differ from a plain program's by a relative error of at most 0.00026.
Values sent between devices are 32-bit elements; how exact they have to be, the bound alone decides.
No kernel may reach another device: no remote copies, remote signals or barrier semaphores. Data moves between devices by JAX's collectives and lax.ppermute only.
A program may use at most 128 MiB of HBM per device.

v0:
```python
import functools
import math

import jax
import jax.numpy as jnp
from jax import lax
from jax.experimental import pallas as pl
from jax.experimental.pallas import tpu as pltpu
from jax.sharding import PartitionSpec as P

K = 64
SWEEPS = 4
HALF = K // 2
TURNS = 8
STEPS = 4
LANES = 128
PARTS = 1
PITCH = 9
PINNED = 1e30
VMEM_BYTES = 16 * 1024 * 1024
PACK_VMEM_BYTES = 50 * 1024 * 1024


def vmem():
    return pl.BlockSpec(memory_space=pltpu.VMEM)


def smem():
    return pl.BlockSpec(memory_space=pltpu.SMEM)


def hbm():
    return pl.BlockSpec(memory_space=pltpu.HBM)


def anywhere():
    return pl.BlockSpec(memory_space=pl.ANY)


def params():
    return pltpu.CompilerParams(vmem_limit_bytes=VMEM_BYTES)


def cost(flops, nbytes):
    return pl.CostEstimate(flops=flops, bytes_accessed=nbytes, transcendentals=0)


def shape_of(*shape):
    return jax.ShapeDtypeStruct(shape, jnp.float32)


def column_parity(rows, columns):
    return lax.broadcasted_iota(jnp.int32, (rows, columns), 1) % 2


def chunks(columns):
    return [(c, pl.ds(LANES * c, LANES)) for c in range(columns // LANES)]


def position():
    gx, gz = lax.axis_index("gx"), lax.axis_index("gz")
    nx, nz = lax.axis_size("gx"), lax.axis_size("gz")
    core = gz % 2
    far = jnp.where(core == 0, gz > 0, gz < nz - 1)
    return core, gx % 2, far, gx > 0, gx < nx - 1


def sends(ref, colour, core, odd, ze_ref, xo_ref, xe_ref, zi_ref):
    planes, rows, columns = ref.shape
    count = columns // LANES
    parity = column_parity(8, LANES)

    def sides(low_ref, high_ref, above_ref, below_ref):
        for j in range(0, rows, 8):
            for _, at in chunks(columns):
                low_ref[pl.ds(j, 8), at] = ref[0, pl.ds(j, 8), at]
                high_ref[pl.ds(j, 8), at] = ref[planes - 1, pl.ds(j, 8), at]
        for k in range(planes // 2):
            for c, at in chunks(columns):
                line = pl.ds(k * count + c, 1)
                last = [ref[2 * k + i, pl.ds(rows - 8, 8), at] for i in (0, 1)]
                first = [ref[2 * k + i, pl.ds(0, 8), at] for i in (0, 1)]
                above_ref[line, :] = jnp.where(parity == 1 - colour, last[0], last[1])[7:8]
                below_ref[line, :] = jnp.where(parity == colour, first[0], first[1])[0:1]

    for c in (0, 1):
        for o in (0, 1):

            @pl.when((core == c) & (odd == o))
            def _():
                z_refs = (zi_ref, ze_ref) if c else (ze_ref, zi_ref)
                x_refs = (xo_ref, xe_ref) if o else (xe_ref, xo_ref)
                sides(*z_refs, *x_refs)


def spread_rows(source, tiles, even):
    for j in range(tiles):
        a = source[pl.ds(2 * j, 8, stride=2 * tiles), :]
        b = source[pl.ds(2 * j + 1, 8, stride=2 * tiles), :]
        yield pl.ds(8 * j, 8), jnp.where(even, a, b), jnp.where(even, b, a)


def pack_kernel(pot_hbm, reg_hbm, lev_hbm, f0_ref, f1_ref, m0_ref, m1_ref, ze_ref, xo_ref, xe_ref, zi_ref, lev_ref,
                pot_ref, reg_ref, field, mark, lev_sem, sems):
    planes, rows, columns = f0_ref.shape
    lev_copy = pltpu.make_async_copy(lev_hbm, lev_ref, lev_sem)
    lev_copy.start()
    copies = [
        [
            pltpu.make_async_copy(source.at[z], target.at[z], sems.at[z, i])
            for i, (source, target) in enumerate(((reg_hbm, reg_ref), (pot_hbm, pot_ref)))
        ]
        for z in range(planes)
    ]
    for plane in copies:
        for copy in plane:
            copy.start()
    lev_copy.wait()
    lane = lax.broadcasted_iota(jnp.int32, (8, LANES), 1)
    table = jnp.zeros((8, LANES), jnp.float32)
    for region in range(1, lev_ref.shape[0]):
        table = jnp.where(lane == region, lev_ref[region], table)
    for z in range(planes):
        even = column_parity(8, LANES) == z % 2
        for copy in copies[z]:
            copy.wait()
        for c, at in chunks(columns):
            slot = z % 2 * (columns // LANES) + c
            for j in range(0, 2 * rows, 8):
                to = pl.ds(j, 8)
                region = reg_ref[z, to, at]
                pinned = jnp.take_along_axis(table, region, axis=1)
                free = region == 0
                field[slot, to, :] = jnp.where(free, pot_ref[z, to, at], pinned)
                mark[slot, to, :] = jnp.where(free, 0.0, PINNED)
            for source, out0, out1 in ((field, f0_ref, f1_ref), (mark, m0_ref, m1_ref)):
                for to, a, b in spread_rows(source.at[slot], rows // 8, even):
                    out0[z, to, at] = a
                    out1[z, to, at] = b
    sends(f1_ref, 1, *position()[:2], ze_ref, xo_ref, xe_ref, zi_ref)


def send_shapes(planes, rows, columns):
    side, line = shape_of(rows, columns), shape_of(planes // 2 * columns // LANES, LANES)
    return [side, line, line, side]


def pack(potential, regions, levels):
    planes, rows, columns = potential.shape
    half = shape_of(planes, rows // 2, columns)
    whole = (planes, rows, columns)
    stage = pltpu.VMEM((2 * columns // LANES, rows, LANES), jnp.float32)
    return pl.pallas_call(
        pack_kernel,
        in_specs=[hbm()] * 3,
        out_specs=[vmem()] * 8,
        out_shape=[half] * 4 + send_shapes(*half.shape),
        scratch_shapes=[
            pltpu.SMEM(levels.shape, jnp.float32),
            pltpu.VMEM(whole, jnp.float32),
            pltpu.VMEM(whole, jnp.int32),
            stage,
            stage,
            pltpu.SemaphoreType.DMA,
            pltpu.SemaphoreType.DMA((planes, 2)),
        ],
        compiler_params=pltpu.CompilerParams(vmem_limit_bytes=PACK_VMEM_BYTES),
        cost_estimate=cost(20 * potential.size, 8 * potential.size),
        name="pack",
    )(potential, regions, levels)


def charge_kernel(chg_hbm, m0_ref, m1_ref, after, c0_ref, c1_ref, done_ref, chg_ref, stage, sems):
    del after
    done_ref[...] = jnp.zeros_like(done_ref)
    planes, rows, columns = m0_ref.shape
    copies = [pltpu.make_async_copy(chg_hbm.at[z], chg_ref.at[z], sems.at[z]) for z in range(planes)]
    for copy in copies:
        copy.start()
    for z in range(planes):
        even = column_parity(8, LANES) == z % 2
        copies[z].wait()
        for c, at in chunks(columns):
            slot = z % 2 * (columns // LANES) + c
            for j in range(0, 2 * rows, 8):
                stage[slot, pl.ds(j, 8), :] = chg_ref[z, pl.ds(j, 8), at]
            for to, a, b in spread_rows(stage.at[slot], rows // 8, even):
                c0_ref[z, to, at] = m0_ref[z, to, at] + a
                c1_ref[z, to, at] = m1_ref[z, to, at] + b


def pack_charge(charge, marks, after):
    planes, rows, columns = charge.shape
    half = shape_of(planes, rows // 2, columns)
    return pl.pallas_call(
        charge_kernel,
        in_specs=[hbm(), vmem(), vmem(), anywhere()],
        out_specs=[vmem()] * 3,
        out_shape=[half, half, shape_of(8, LANES)],
        scratch_shapes=[
            pltpu.VMEM(charge.shape, jnp.float32),
            pltpu.VMEM((2 * columns // LANES, rows, LANES), jnp.float32),
            pltpu.SemaphoreType.DMA((planes,)),
        ],
        compiler_params=pltpu.CompilerParams(vmem_limit_bytes=PACK_VMEM_BYTES),
        cost_estimate=cost(20 * charge.size, 4 * charge.size),
        name="charge",
    )(charge, *marks, after)


def relax(own_ref, other_ref, charge_ref, ze_ref, xo_ref, xe_ref, zi_ref, below, above, colour, put):
    core, odd, far_live, below_live, above_live = position()
    planes, rows, columns = own_ref.shape
    tiles, count = rows // 8, columns // LANES
    row = lax.broadcasted_iota(jnp.int32, (8, LANES), 0)
    lane = lax.broadcasted_iota(jnp.int32, (8, LANES), 1)
    parity = column_parity(8, LANES)
    xe, xo = xe_ref[...], xo_ref[...]
    below[...] = jnp.where(below_live, jnp.where(odd == 0, xo, xe), 0.0)
    above[...] = jnp.where(above_live, jnp.where(odd == 0, xe, xo), 0.0)

    for z in range(planes):
        first_row = parity == (z + colour) % 2
        for j in range(tiles):
            rows_at = pl.ds(8 * j, 8)
            for c, at in chunks(columns):
                tile = lambda t, at=at: other_ref[z, pl.ds(8 * t, 8), at]
                mid = tile(j)
                if z in (0, planes - 1):
                    far = jnp.where(far_live, ze_ref[rows_at, at], 0.0)
                    near = zi_ref[rows_at, at]
                z_low = other_ref[z - 1, rows_at, at] if z else jnp.where(core == 0, far, near)
                z_high = other_ref[z + 1, rows_at, at] if z < planes - 1 else jnp.where(core == 0, near, far)
                line = pl.ds(z // 2 * count + c, 1)
                if j:
                    x_low = tile(j - 1)
                else:
                    x_low = jnp.where(row == 0, below[line, :], pltpu.roll(tile(tiles - 1), 1, 0))
                if j < tiles - 1:
                    x_high = tile(j + 1)
                else:
                    x_high = jnp.where(row == 7, above[line, :], pltpu.roll(tile(0), 7, 0))
                left = other_ref[z, rows_at, pl.ds(LANES * (c - 1), LANES)] if c else 0.0
                right = other_ref[z, rows_at, pl.ds(LANES * (c + 1), LANES)] if c < count - 1 else 0.0
                y_low = pltpu.roll(jnp.where(lane == LANES - 1, left, mid), 1, 1)
                y_high = pltpu.roll(jnp.where(lane == 0, right, mid), LANES - 1, 1)
                charge = charge_ref[z, rows_at, at]
                beside = z_low + z_high + mid + jnp.where(first_row, x_low, x_high) + y_low + y_high
                own = own_ref[z, rows_at, at]
                put(z, j, c, jnp.where(charge < PINNED, 0.25 * (beside + charge) - 0.5 * own, own))


def line_scratch(planes, columns):
    return [pltpu.VMEM((planes // 2 * columns // LANES, LANES), jnp.float32)] * 2


def relax_kernel(colour, own_ref, other_ref, charge_ref, ze_ref, xo_ref, xe_ref, zi_ref, after,
                 out_ref, ze_out, xo_out, xe_out, zi_out, below, above):
    del after

    def put(z, j, c, value):
        out_ref[z, pl.ds(8 * j, 8), pl.ds(LANES * c, LANES)] = value

    relax(own_ref, other_ref, charge_ref, ze_ref, xo_ref, xe_ref, zi_ref, below, above, colour, put)
    sends(out_ref, colour, *position()[:2], ze_out, xo_out, xe_out, zi_out)


def half_sweep(own, other, charge, halos, colour, after):
    return pl.pallas_call(
        functools.partial(relax_kernel, colour),
        in_specs=[vmem()] * 7 + [anywhere()],
        out_specs=[vmem()] * 5,
        out_shape=[shape_of(*own.shape)] + send_shapes(*own.shape),
        scratch_shapes=line_scratch(own.shape[0], own.shape[2]),
        compiler_params=params(),
        cost_estimate=cost(14 * own.size, 0),
        name="relax",
    )(own, other, charge, *halos, after)


def split(value):
    high = value.astype(jnp.bfloat16)
    return high, (value - high.astype(jnp.float32)).astype(jnp.bfloat16)


def angles_kernel(rows_total, tiles, columns, offset, after, left_ref, radial_ref, done_ref, terms_ref):
    del after
    done_ref[...] = jnp.zeros_like(done_ref)
    shape = (8, columns)
    column = lax.broadcasted_iota(jnp.int32, shape, 1)
    v = (column.astype(jnp.float32) + 0.5) * (2.0 / columns) - 1.0
    for j in range(tiles):
        packed = lax.broadcasted_iota(jnp.int32, shape, 0) * tiles + j
        row = lax.axis_index("gx") * (16 * tiles) + 2 * packed + (column + offset) % 2
        u = (row.astype(jnp.float32) + 0.5) * (2.0 / rows_total) - 1.0
        inverse = lax.rsqrt(u * u + v * v)
        c1, s1 = u * inverse, v * inverse
        c2, s2 = c1 * c1 - s1 * s1, 2.0 * (c1 * s1)
        c4, s4 = c2 * c2 - s2 * s2, 2.0 * (c2 * s2)
        u2, v2 = u * c1 - v * s1, u * s1 + v * c1
        u3, v3 = u2 * c1 - v2 * s1, u2 * s1 + v2 * c1
        u4, v4 = u2 * c2 - v2 * s2, u2 * s2 + v2 * c2
        for m, value in enumerate((u, u2, u3, u4, v, v2, v3, v4)):
            radial_ref[j, pl.ds(8 * m, 8), :] = value

        def put(index, pair):
            high, low = split(jnp.concatenate(pair, axis=0))
            terms_ref[pl.ds(8 * index, 16), :] = high
            terms_ref[pl.ds(8 * (2 * TURNS + index), 16), :] = low

        twice = 2.0 * c4
        cosines, sines = [jnp.ones_like(c4), c4], [jnp.zeros_like(c4), s4]
        for a in range(0, TURNS, 2):
            put(a, cosines)
            put(TURNS + a, sines)
            for terms in (cosines, sines):
                terms[0] = twice * terms[1] - terms[0]
                terms[1] = twice * terms[0] - terms[1]
        left_ref[j] = terms_ref[...].T


def angles(after, rows_total, tiles, columns, offset):
    left = jax.ShapeDtypeStruct((tiles, columns, 32 * TURNS), jnp.bfloat16)
    return pl.pallas_call(
        functools.partial(angles_kernel, rows_total, tiles, columns, offset),
        in_specs=[anywhere()],
        out_specs=[vmem()] * 3,
        out_shape=[left, shape_of(tiles, 16 * STEPS, columns), shape_of(8, LANES)],
        scratch_shapes=[pltpu.VMEM((32 * TURNS, columns), jnp.bfloat16)],
        compiler_params=params(),
        cost_estimate=cost(128 * tiles * 8 * columns, 0),
        name="angles",
    )(after)


def multipoles_of(colour, field_of, tables, planes, right):
    outs = [None] * planes
    pairs = planes // 2
    n, m = 16 * TURNS, 16 * STEPS * pairs
    tiles = tables[0][0].shape[0]
    for e in (0, 1):
        left_ref, radial_ref = tables[e]
        total = None
        for j in range(tiles):
            slot = (e * tiles + j) % right.shape[0]
            for k in range(pairs):
                f = field_of(2 * k + (e + colour) % 2, j)
                twice = jnp.concatenate([f, f], axis=0)
                for b in range(0, 2 * STEPS, 2):
                    high, low = split(twice * radial_ref[j, pl.ds(8 * b, 16), :])
                    index = 2 * STEPS * k + b
                    right[slot, pl.ds(8 * index, 16), :] = high
                    right[slot, pl.ds(m + 8 * index, 16), :] = low
            product = jnp.dot(right[slot], left_ref[j], preferred_element_type=jnp.float32)
            total = product if total is None else total + product
        total = ((total[:m, :n] + total[m:, :n]) + (total[:m, n:] + total[m:, n:])).T
        i = lax.broadcasted_iota(jnp.int32, total.shape, 0)
        k = lax.broadcasted_iota(jnp.int32, total.shape, 1)
        total = jnp.sum(jnp.where(i % 8 == k % 8, total, 0.0).reshape(2 * TURNS, 8, m), axis=1)
        for shift in (1, 2, 4):
            total = total + pltpu.roll(total, shift, 1)
        half = 8 * STEPS
        even, odd = total[:TURNS], total[TURNS:]
        cosines = even - pltpu.roll(odd, m - half, 1)
        sines = odd + pltpu.roll(even, m - half, 1)
        lane = lax.broadcasted_iota(jnp.int32, (TURNS, m), 1)
        total = jnp.where(lane // half % 2 == 0, cosines, pltpu.roll(sines, half, 1))
        for k in range(pairs):
            outs[2 * k + (e + colour) % 2] = total[:, 2 * half * k : 2 * half * (k + 1)]
    return jnp.concatenate(outs, axis=1)


def right_scratch(planes, columns):
    return pltpu.VMEM((2, 16 * STEPS * planes, columns), jnp.bfloat16)


def sums_shape(planes):
    return shape_of(TURNS, 16 * STEPS * planes)


def multipole_kernel(field_ref, left0, radial0, left1, radial1, out_ref, done_ref, right):
    done_ref[...] = jnp.zeros_like(done_ref)
    out_ref[...] = multipoles_of(
        0,
        lambda z, j: field_ref[z, pl.ds(8 * j, 8), :],
        ((left0, radial0), (left1, radial1)),
        field_ref.shape[0],
        right,
    )


def multipole_sums(field, tables):
    planes, _, columns = field.shape
    return pl.pallas_call(
        multipole_kernel,
        in_specs=[vmem()] * 5,
        out_specs=[vmem()] * 2,
        out_shape=[sums_shape(planes), shape_of(8, LANES)],
        scratch_shapes=[right_scratch(planes, columns)],
        compiler_params=params(),
        cost_estimate=cost(100 * field.size, 0),
        name="multipole",
    )(field, *tables)


def last_kernel(scale, own_ref, other_ref, charge_ref, ze_ref, xo_ref, xe_ref, zi_ref, left0, radial0, left1,
                radial1, sums_ref, after, field_hbm, out_ref, one, staged, right, below, above, sems):
    del after
    planes, rows, columns = own_ref.shape
    tiles = rows // 8
    copies = []

    def put(z, j, c, value):
        at = pl.ds(LANES * c, LANES)
        one[z, pl.ds(8 * j, 8), at] = value
        even = column_parity(8, LANES) == z % 2
        zero = other_ref[z, pl.ds(8 * j, 8), at]
        staged[z, c, pl.ds(2 * j, 8, stride=2 * tiles), :] = jnp.where(even, zero, value)
        staged[z, c, pl.ds(2 * j + 1, 8, stride=2 * tiles), :] = jnp.where(even, value, zero)
        if j == tiles - 1:
            copy = pltpu.make_async_copy(staged.at[z, c], field_hbm.at[z, :, at], sems.at[z, c])
            copy.start()
            copies.append(copy)

    relax(own_ref, other_ref, charge_ref, ze_ref, xo_ref, xe_ref, zi_ref, below, above, 1, put)
    sums = multipoles_of(
        1, lambda z, j: one[z, pl.ds(8 * j, 8), :], ((left0, radial0), (left1, radial1)), planes, right
    )
    out_ref[...] = (sums + sums_ref[...]) * scale
    for copy in copies:
        copy.wait()


def last_half_sweep(own, other, charge, halos, tables, sums, after, scale):
    planes, rows, columns = own.shape
    return pl.pallas_call(
        functools.partial(last_kernel, scale),
        in_specs=[vmem()] * 12 + [anywhere()],
        out_specs=[hbm(), vmem()],
        out_shape=[shape_of(planes, 2 * rows, columns), sums_shape(planes)],
        scratch_shapes=[
            pltpu.VMEM(own.shape, jnp.float32),
            pltpu.VMEM((planes, columns // LANES, 2 * rows, LANES), jnp.float32),
            right_scratch(planes, columns),
            *line_scratch(planes, columns),
            pltpu.SemaphoreType.DMA((planes, columns // LANES)),
        ],
        compiler_params=params(),
        cost_estimate=cost(100 * own.size, 0),
        name="relax_last",
    )(own, other, charge, *halos, *tables, sums, after)


def swaps(pairs):
    return [(a, b) for a, b in pairs] + [(b, a) for a, b in pairs]


def far_pairs(nx, nz):
    step = nx // 4
    pairs = [(x * nz + z, x * nz + z + 1) for x in range(nx) for z in range(1, nz - 1, 2)]
    ends = [x for x in range(nx) if x // step % 2 == 0]
    return swaps(pairs + [(x * nz + z, (x + step) * nz + z) for x in ends for z in (0, nz - 1)])


def odd_pairs(nx, nz):
    pairs = [(x * nz + z, (x + 1) * nz + z) for x in range(1, nx - 1, 2) for z in range(nz)]
    return swaps(pairs + [(x * nz + z, x * nz + z + 1) for x in (0, nx - 1) for z in range(0, nz, 2)])


def local(potential, regions, charge, levels):
    planes, row_count, columns = potential.shape
    nx, nz = lax.axis_size("gx"), lax.axis_size("gz")
    rows_total = nx * row_count
    tiles = row_count // 16
    z_near, x_even = [(i, i ^ 1) for i in range(nz)], [(i, i ^ 1) for i in range(nx)]
    z_far, x_odd = far_pairs(nx, nz), odd_pairs(nx, nz)

    def exchange(ze, xo, xe, zi):
        ze = lax.ppermute(ze, ("gx", "gz"), z_far)
        xo = lax.ppermute(xo, ("gx", "gz"), x_odd)
        xe = lax.ppermute(xe, "gx", x_even)
        zi = lax.ppermute(zi, "gz", z_near)
        return ze, xo, xe, zi

    zero, one, *rest = pack(potential, regions, levels)
    marks, out = rest[:2], rest[2:]
    charge0, charge1, after = pack_charge(charge, marks, out[1])
    tables = []
    for sweep in range(SWEEPS):
        halos = exchange(*out)
        zero, *out = half_sweep(zero, one, charge0, halos, 0, after)
        halos = exchange(*out)
        after = zero
        if sweep < SWEEPS - 1:
            if sweep < 2:
                *table, after = angles(out[1], rows_total, tiles, columns, sweep)
                tables += table
            one, *out = half_sweep(one, zero, charge1, halos, 1, after)
            after = one
    sums, after = multipole_sums(zero, tables)
    scale = 1.0 / math.sqrt(rows_total * columns)
    field, sums = last_half_sweep(one, zero, charge1, halos, tables, sums, after, scale)
    share = K // nx
    parts = jnp.transpose(sums[:, 7::8].reshape(TURNS, planes, 2, STEPS), (1, 2, 0, 3)).reshape(planes, nx, share)
    parts = jnp.transpose(parts, (1, 0, 2)).reshape(nx, planes * share)
    shares = lax.all_to_all(parts, "gx", 0, 0, tiled=True)
    return field, jnp.sum(shares, axis=0).reshape(planes, share)


def solution(mesh):
    in_specs = (P("gz", "gx", None), P("gz", "gx", None), P("gz", "gx", None), P())
    out_specs = (P("gz", "gx", None), P("gz", "gx"))
    return jax.shard_map(local, mesh=mesh, in_specs=in_specs, out_specs=out_specs, check_vma=False)
```

profile of v0, /device:TPU:8, one launch (start us, length us, event | category | flops | bytes accessed | tf_op | source)
XLA Modules:
  0.0 93.9 jit_solution(14816267098583781194)
XLA Ops:
  0.6 0.6 copy-done
  1.3 4.3 %pack.1 = (f32[4,32,2048]{2,1,0:T(8,128)S(1)}, f32[4,32,2048]{2,1,0:T(8,128)S(1)}, f32[4,32,2048]{2,1,0:T(8,128)S(1)}, f32[4,32,2048]{2,1,0:T(8,128)}, f32[32,20...) custom-call(f32[4,64,2048]{2,1,0:T(8,128)} %pot_hbm.1, ...), custom_call_target="tpu_custom_call" | custom-call | flops 10485760 | bytes 4194304 | tf_op jit(solution)/shard_map/pack/pallas_call | solution.py:153
  5.6 0.1 collective-permute-start
  5.7 1.7 %collective-permute-start.3 = (f32[32,2048]{1,0:T(8,128)S(1)}, f32[32,2048]{1,0:T(8,128)S(1)}, u32[]{:S(2)}, u32[]{:S(2)}) collective-permute-start(f32[32,2048]{1,0:T(8,128)S(1)} %get-tuple-element.66), channel_id=1, source_target_pairs={{0,1},{1,0},{2,3},{3,2},{4,5},{5,4},{6,7},{7,6},{8,9},{9,8},{10,11... | collective-permute-start | bytes 786440 | tf_op jit(solution)/shard_map/ppermute | solution.py:482
  7.3 1.9 %collective-permute-start.2 = (f32[32,128]{1,0:T(8,128)S(1)}, f32[32,128]{1,0:T(8,128)S(1)}, u32[]{:S(2)}, u32[]{:S(2)}) collective-permute-start(f32[32,128]{1,0:T(8,128)S(1)} %get-tuple-element.65), channel_id=1, source_target_pairs={{0,8},{8,0},{16,24},{24,16},{32,40},{40,32},{48,56},{56,48},{64,72... | collective-permute-start | bytes 49160 | tf_op jit(solution)/shard_map/ppermute | solution.py:481
  9.2 3.0 %charge.1 = (f32[4,32,2048]{2,1,0:T(8,128)S(1)}, f32[4,32,2048]{2,1,0:T(8,128)S(1)}, f32[8,128]{1,0:T(8,128)S(1)}) custom-call(f32[4,64,2048]{2,1,0:T(8,128)} %chg_hbm.1, f32[4,32,2048]{2,1,0:T(8,128)S(1)} %get-tuple-element.60.m0_ref, f32[4,32,2048]{2,1,0:T(8,128)} %get-tuple-element.61.m1_ref, f32[32,128]{1,0:T(8,128)S(1)} %get-tuple-element.62.after), custom_call_target="tpu_custom_call" | custom-call | flops 10485760 | bytes 2097152 | tf_op jit(solution)/shard_map/charge/pallas_call | solution.py:195
  12.3 0.8 relax.7
  13.1 0.6 collective-permute-start.4
  13.7 0.8 collective-permute-start.7
  14.5 3.8 %collective-permute-start.6 = (f32[32,128]{1,0:T(8,128)S(1)}, f32[32,128]{1,0:T(8,128)S(1)}, u32[]{:S(2)}, u32[]{:S(2)}) collective-permute-start(f32[32,128]{1,0:T(8,128)S(1)} %get-tuple-element.72), channel_id=1, source_target_pairs={{0,8},{8,0},{16,24},{24,16},{32,40},{40,32},{48,56},{56,48},{64,72... | collective-permute-start | bytes 49160 | tf_op jit(solution)/shard_map/ppermute | solution.py:481
  18.4 1.4 %angles.2 = (bf16[4,2048,256]{2,1,0:T(8,128)(2,1)S(1)}, f32[4,64,2048]{2,1,0:T(8,128)S(1)}, f32[8,128]{1,0:T(8,128)S(1)}) custom-call(f32[32,128]{1,0:T(8,128)S(1)} %get-tuple-element.71.after), custom_call_target="tpu_custom_call" | custom-call | flops 8388608 | tf_op jit(solution)/shard_map/angles/pallas_call | solution.py:324
  19.8 0.3 collective-permute-done.6.xe_ref
  20.1 0.7 relax.8
  20.9 3.0 %collective-permute-start.8 = (f32[32,2048]{1,0:T(8,128)S(1)}, f32[32,2048]{1,0:T(8,128)S(1)}, u32[]{:S(2)}, u32[]{:S(2)}) collective-permute-start(f32[32,2048]{1,0:T(8,128)S(1)} %get-tuple-element.76), channel_id=1, source_target_pairs={{1,2},{3,4},{5,6},{9,10},{11,12},{13,14},{17,18},{19,20},{21,22},{... | collective-permute-start | bytes 786440 | tf_op jit(solution)/shard_map/ppermute | solution.py:479
  23.9 0.5 collective-permute-start.9
  24.4 3.8 %collective-permute-start.10 = (f32[32,128]{1,0:T(8,128)S(1)}, f32[32,128]{1,0:T(8,128)S(1)}, u32[]{:S(2)}, u32[]{:S(2)}) collective-permute-start(f32[32,128]{1,0:T(8,128)S(1)} %get-tuple-element.78), channel_id=1, source_target_pairs={{0,8},{8,0},{16,24},{24,16},{32,40},{40,32},{48,56},{56,48},{64,72... | collective-permute-start | bytes 49160 | tf_op jit(solution)/shard_map/ppermute | solution.py:481
  28.2 1.7 %collective-permute-done.10.xe_ref = f32[32,128]{1,0:T(8,128)S(1)} collective-permute-done((f32[32,128]{1,0:T(8,128)S(1)}, f32[32,128]{1,0:T(8,128)S(1)}, u32[]{:S(2)}, u32[]{:S(2)}) %collective-permute-start.10) | collective-permute-done | bytes 16416 | tf_op jit(solution)/shard_map/ppermute | solution.py:481
  29.9 0.8 relax.9
  30.7 1.6 %collective-permute-start.12 = (f32[32,2048]{1,0:T(8,128)S(1)}, f32[32,2048]{1,0:T(8,128)S(1)}, u32[]{:S(2)}, u32[]{:S(2)}) collective-permute-start(f32[32,2048]{1,0:T(8,128)S(1)} %get-tuple-element.81), channel_id=1, source_target_pairs={{1,2},{3,4},{5,6},{9,10},{11,12},{13,14},{17,18},{19,20},{21,22},{... | collective-permute-start | bytes 786440 | tf_op jit(solution)/shard_map/ppermute | solution.py:479
  32.3 0.8 collective-permute-start.14
  33.2 1.4 %angles.3 = (bf16[4,2048,256]{2,1,0:T(8,128)(2,1)S(1)}, f32[4,64,2048]{2,1,0:T(8,128)S(1)}, f32[8,128]{1,0:T(8,128)S(1)}) custom-call(f32[32,128]{1,0:T(8,128)S(1)} %get-tuple-element.82.after), custom_call_target="tpu_custom_call" | custom-call | flops 8388608 | tf_op jit(solution)/shard_map/angles/pallas_call | solution.py:324
  34.6 1.5 %collective-permute-done.14.xe_ref = f32[32,128]{1,0:T(8,128)S(1)} collective-permute-done((f32[32,128]{1,0:T(8,128)S(1)}, f32[32,128]{1,0:T(8,128)S(1)}, u32[]{:S(2)}, u32[]{:S(2)}) %collective-permute-start.14) | collective-permute-done | bytes 16416 | tf_op jit(solution)/shard_map/ppermute | solution.py:481
  36.1 0.5 collective-permute-done.12.ze_ref
  36.6 0.8 relax.10
  37.4 3.8 %collective-permute-start.16 = (f32[32,2048]{1,0:T(8,128)S(1)}, f32[32,2048]{1,0:T(8,128)S(1)}, u32[]{:S(2)}, u32[]{:S(2)}) collective-permute-start(f32[32,2048]{1,0:T(8,128)S(1)} %get-tuple-element.87), channel_id=1, source_target_pairs={{1,2},{3,4},{5,6},{9,10},{11,12},{13,14},{17,18},{19,20},{21,22},{... | collective-permute-start | bytes 786440 | tf_op jit(solution)/shard_map/ppermute | solution.py:479
  41.2 0.5 collective-permute-start.17
  41.7 1.5 %collective-permute-start.18 = (f32[32,128]{1,0:T(8,128)S(1)}, f32[32,128]{1,0:T(8,128)S(1)}, u32[]{:S(2)}, u32[]{:S(2)}) collective-permute-start(f32[32,128]{1,0:T(8,128)S(1)} %get-tuple-element.89), channel_id=1, source_target_pairs={{0,8},{8,0},{16,24},{24,16},{32,40},{40,32},{48,56},{56,48},{64,72... | collective-permute-start | bytes 49160 | tf_op jit(solution)/shard_map/ppermute | solution.py:481
  43.3 2.2 %collective-permute-done.18.xe_ref = f32[32,128]{1,0:T(8,128)S(1)} collective-permute-done((f32[32,128]{1,0:T(8,128)S(1)}, f32[32,128]{1,0:T(8,128)S(1)}, u32[]{:S(2)}, u32[]{:S(2)}) %collective-permute-start.18) | collective-permute-done | bytes 16416 | tf_op jit(solution)/shard_map/ppermute | solution.py:481
  45.5 0.8 relax.11
  46.3 2.6 %collective-permute-start.20 = (f32[32,2048]{1,0:T(8,128)S(1)}, f32[32,2048]{1,0:T(8,128)S(1)}, u32[]{:S(2)}, u32[]{:S(2)}) collective-permute-start(f32[32,2048]{1,0:T(8,128)S(1)} %get-tuple-element.92), channel_id=1, source_target_pairs={{1,2},{3,4},{5,6},{9,10},{11,12},{13,14},{17,18},{19,20},{21,22},{... | collective-permute-start | bytes 786440 | tf_op jit(solution)/shard_map/ppermute | solution.py:479
  48.9 0.5 collective-permute-start.21
  49.5 1.1 %collective-permute-start.22 = (f32[32,128]{1,0:T(8,128)S(1)}, f32[32,128]{1,0:T(8,128)S(1)}, u32[]{:S(2)}, u32[]{:S(2)}) collective-permute-start(f32[32,128]{1,0:T(8,128)S(1)} %get-tuple-element.94), channel_id=1, source_target_pairs={{0,8},{8,0},{16,24},{24,16},{32,40},{40,32},{48,56},{56,48},{64,72... | collective-permute-start | bytes 49160 | tf_op jit(solution)/shard_map/ppermute | solution.py:481
  50.6 2.6 %collective-permute-done.22.xe_ref = f32[32,128]{1,0:T(8,128)S(1)} collective-permute-done((f32[32,128]{1,0:T(8,128)S(1)}, f32[32,128]{1,0:T(8,128)S(1)}, u32[]{:S(2)}, u32[]{:S(2)}) %collective-permute-start.22) | collective-permute-done | bytes 16416 | tf_op jit(solution)/shard_map/ppermute | solution.py:481
  53.2 0.7 relax.12
  53.9 3.0 %collective-permute-start.24 = (f32[32,2048]{1,0:T(8,128)S(1)}, f32[32,2048]{1,0:T(8,128)S(1)}, u32[]{:S(2)}, u32[]{:S(2)}) collective-permute-start(f32[32,2048]{1,0:T(8,128)S(1)} %get-tuple-element.97), channel_id=1, source_target_pairs={{1,2},{3,4},{5,6},{9,10},{11,12},{13,14},{17,18},{19,20},{21,22},{... | collective-permute-start | bytes 786440 | tf_op jit(solution)/shard_map/ppermute | solution.py:479
  56.9 0.5 collective-permute-start.25
  57.4 1.2 %collective-permute-start.26 = (f32[32,128]{1,0:T(8,128)S(1)}, f32[32,128]{1,0:T(8,128)S(1)}, u32[]{:S(2)}, u32[]{:S(2)}) collective-permute-start(f32[32,128]{1,0:T(8,128)S(1)} %get-tuple-element.99), channel_id=1, source_target_pairs={{0,8},{8,0},{16,24},{24,16},{32,40},{40,32},{48,56},{56,48},{64,72... | collective-permute-start | bytes 49160 | tf_op jit(solution)/shard_map/ppermute | solution.py:481
  58.6 2.5 %collective-permute-done.26.xe_ref = f32[32,128]{1,0:T(8,128)S(1)} collective-permute-done((f32[32,128]{1,0:T(8,128)S(1)}, f32[32,128]{1,0:T(8,128)S(1)}, u32[]{:S(2)}, u32[]{:S(2)}) %collective-permute-start.26) | collective-permute-done | bytes 16416 | tf_op jit(solution)/shard_map/ppermute | solution.py:481
  61.1 0.7 relax.13
  61.8 3.3 %collective-permute-start.28 = (f32[32,2048]{1,0:T(8,128)S(1)}, f32[32,2048]{1,0:T(8,128)S(1)}, u32[]{:S(2)}, u32[]{:S(2)}) collective-permute-start(f32[32,2048]{1,0:T(8,128)S(1)} %get-tuple-element.102), channel_id=1, source_target_pairs={{1,2},{3,4},{5,6},{9,10},{11,12},{13,14},{17,18},{19,20},{21,22},{... | collective-permute-start | bytes 786440 | tf_op jit(solution)/shard_map/ppermute | solution.py:479
  65.2 0.5 collective-permute-start.29
  65.7 0.9 %collective-permute-start.30 = (f32[32,128]{1,0:T(8,128)S(1)}, f32[32,128]{1,0:T(8,128)S(1)}, u32[]{:S(2)}, u32[]{:S(2)}) collective-permute-start(f32[32,128]{1,0:T(8,128)S(1)} %get-tuple-element.104), channel_id=1, source_target_pairs={{0,8},{8,0},{16,24},{24,16},{32,40},{40,32},{48,56},{56,48},{64,72... | collective-permute-start | bytes 49160 | tf_op jit(solution)/shard_map/ppermute | solution.py:481
  66.6 2.9 %multipole.1 = (f32[8,256]{1,0:T(8,128)S(1)}, f32[8,128]{1,0:T(8,128)S(1)}) custom-call(f32[4,32,2048]{2,1,0:T(8,128)S(1)} %get-tuple-element.101.field_ref.other_ref, bf16[4,2048,256]{2,1,0:T(8,128)(2,1)S(1)} %get-tuple-element.106.left0, f32[4,64,2048]{2,1,0:T(8,128)S(1)} %get-tuple-element.107.radial0, ...), custom_call_target="tpu_custom_call" | custom-call | flops 26214400 | tf_op jit(solution)/shard_map/multipole/pallas_call | solution.py:394
  69.5 4.6 %relax_last.1 = (f32[4,64,2048]{2,1,0:T(8,128)}, f32[8,256]{1,0:T(8,128)S(1)}) custom-call(f32[4,32,2048]{2,1,0:T(8,128)S(1)} %get-tuple-element.96.other_ref.after.own_ref, f32[4,32,2048]{2,1,0:T(8,128)S(1)} %get-tuple-element.101.field_ref.other_ref, f32[4,32,2048]{2,1,0:T(8,128)S(1)} %get-tuple-element.69.charge_ref, ...), custom_call_target="tpu_custom_call" | custom-call | flops 26214400 | tf_op jit(solution)/shard_map/relax_last/pallas_call | solution.py:436
  74.1 0.1 slice.3
  74.3 0.1 copy.12
  74.6 18.5 %all_to_all.9 = f32[32,1,8]{2,1,0:T(1,128)S(1)} all-to-all(f32[32,1,8]{2,1,0:T(1,128)S(1)} %copy.14), channel_id=1, replica_groups=mesh['gx'=32,'gz'=8] {'gx'}, dimensions={0} | all-to-all | bytes 2048 | tf_op jit(solution)/shard_map/all_to_all | solution.py:506
  93.3 0.7 copy.15
  (40 shorter events, 0.5 us)
Async XLA Ops:
  0.6 0.7 copy-start
  5.6 6.7 %collective-permute-start = (f32[32,2048]{1,0:T(8,128)S(1)}, f32[32,2048]{1,0:T(8,128)S(1)}, u32[]{:S(2)}, u32[]{:S(2)}) collective-permute-start(f32[32,2048]{1,0:T(8,128)S(1)} %get-tuple-element.64), channel_id=1, source_target_pairs={{1,2},{3,4},{5,6},{9,10},{11,12},{13,14},{17,18},{19,20},{21,22},{... | collective-permute-start | bytes 786440 | tf_op jit(solution)/shard_map/ppermute | solution.py:479
  5.7 6.6 %collective-permute-start.3 = (f32[32,2048]{1,0:T(8,128)S(1)}, f32[32,2048]{1,0:T(8,128)S(1)}, u32[]{:S(2)}, u32[]{:S(2)}) collective-permute-start(f32[32,2048]{1,0:T(8,128)S(1)} %get-tuple-element.66), channel_id=1, source_target_pairs={{0,1},{1,0},{2,3},{3,2},{4,5},{5,4},{6,7},{7,6},{8,9},{9,8},{10,11... | collective-permute-start | bytes 786440 | tf_op jit(solution)/shard_map/ppermute | solution.py:482
  7.3 4.9 %collective-permute-start.2 = (f32[32,128]{1,0:T(8,128)S(1)}, f32[32,128]{1,0:T(8,128)S(1)}, u32[]{:S(2)}, u32[]{:S(2)}) collective-permute-start(f32[32,128]{1,0:T(8,128)S(1)} %get-tuple-element.65), channel_id=1, source_target_pairs={{0,8},{8,0},{16,24},{24,16},{32,40},{40,32},{48,56},{56,48},{64,72... | collective-permute-start | bytes 49160 | tf_op jit(solution)/shard_map/ppermute | solution.py:481
  9.2 3.0 %collective-permute-start.1 = (f32[32,128]{1,0:T(8,128)S(1)}, f32[32,128]{1,0:T(8,128)S(1)}, u32[]{:S(2)}, u32[]{:S(2)}) collective-permute-start(f32[32,128]{1,0:T(8,128)S(1)} %get-tuple-element.62.after), channel_id=1, source_target_pairs={{8,16},{9,17},{10,18},{11,19},{12,20},{13,21},{14,22},{15,23},{24,... | collective-permute-start | bytes 49160 | tf_op jit(solution)/shard_map/ppermute | solution.py:480
  13.1 7.0 %collective-permute-start.4 = (f32[32,2048]{1,0:T(8,128)S(1)}, f32[32,2048]{1,0:T(8,128)S(1)}, u32[]{:S(2)}, u32[]{:S(2)}) collective-permute-start(f32[32,2048]{1,0:T(8,128)S(1)} %get-tuple-element.70), channel_id=1, source_target_pairs={{1,2},{3,4},{5,6},{9,10},{11,12},{13,14},{17,18},{19,20},{21,22},{... | collective-permute-start | bytes 786440 | tf_op jit(solution)/shard_map/ppermute | solution.py:479
  13.7 6.4 %collective-permute-start.7 = (f32[32,2048]{1,0:T(8,128)S(1)}, f32[32,2048]{1,0:T(8,128)S(1)}, u32[]{:S(2)}, u32[]{:S(2)}) collective-permute-start(f32[32,2048]{1,0:T(8,128)S(1)} %get-tuple-element.73), channel_id=1, source_target_pairs={{0,1},{1,0},{2,3},{3,2},{4,5},{5,4},{6,7},{7,6},{8,9},{9,8},{10,11... | collective-permute-start | bytes 786440 | tf_op jit(solution)/shard_map/ppermute | solution.py:482
  14.5 5.5 %collective-permute-start.6 = (f32[32,128]{1,0:T(8,128)S(1)}, f32[32,128]{1,0:T(8,128)S(1)}, u32[]{:S(2)}, u32[]{:S(2)}) collective-permute-start(f32[32,128]{1,0:T(8,128)S(1)} %get-tuple-element.72), channel_id=1, source_target_pairs={{0,8},{8,0},{16,24},{24,16},{32,40},{40,32},{48,56},{56,48},{64,72... | collective-permute-start | bytes 49160 | tf_op jit(solution)/shard_map/ppermute | solution.py:481
  18.4 1.7 %collective-permute-start.5 = (f32[32,128]{1,0:T(8,128)S(1)}, f32[32,128]{1,0:T(8,128)S(1)}, u32[]{:S(2)}, u32[]{:S(2)}) collective-permute-start(f32[32,128]{1,0:T(8,128)S(1)} %get-tuple-element.71.after), channel_id=1, source_target_pairs={{8,16},{9,17},{10,18},{11,19},{12,20},{13,21},{14,22},{15,23},{24,... | collective-permute-start | bytes 49160 | tf_op jit(solution)/shard_map/ppermute | solution.py:480
  20.9 9.0 %collective-permute-start.8 = (f32[32,2048]{1,0:T(8,128)S(1)}, f32[32,2048]{1,0:T(8,128)S(1)}, u32[]{:S(2)}, u32[]{:S(2)}) collective-permute-start(f32[32,2048]{1,0:T(8,128)S(1)} %get-tuple-element.76), channel_id=1, source_target_pairs={{1,2},{3,4},{5,6},{9,10},{11,12},{13,14},{17,18},{19,20},{21,22},{... | collective-permute-start | bytes 786440 | tf_op jit(solution)/shard_map/ppermute | solution.py:479
  23.9 6.0 %collective-permute-start.11 = (f32[32,2048]{1,0:T(8,128)S(1)}, f32[32,2048]{1,0:T(8,128)S(1)}, u32[]{:S(2)}, u32[]{:S(2)}) collective-permute-start(f32[32,2048]{1,0:T(8,128)S(1)} %get-tuple-element.79), channel_id=1, source_target_pairs={{0,1},{1,0},{2,3},{3,2},{4,5},{5,4},{6,7},{7,6},{8,9},{9,8},{10,11... | collective-permute-start | bytes 786440 | tf_op jit(solution)/shard_map/ppermute | solution.py:482
  23.9 4.3 %collective-permute-start.9 = (f32[32,128]{1,0:T(8,128)S(1)}, f32[32,128]{1,0:T(8,128)S(1)}, u32[]{:S(2)}, u32[]{:S(2)}) collective-permute-start(f32[32,128]{1,0:T(8,128)S(1)} %get-tuple-element.77), channel_id=1, source_target_pairs={{8,16},{9,17},{10,18},{11,19},{12,20},{13,21},{14,22},{15,23},{24,... | collective-permute-start | bytes 49160 | tf_op jit(solution)/shard_map/ppermute | solution.py:480
  24.4 5.5 %collective-permute-start.10 = (f32[32,128]{1,0:T(8,128)S(1)}, f32[32,128]{1,0:T(8,128)S(1)}, u32[]{:S(2)}, u32[]{:S(2)}) collective-permute-start(f32[32,128]{1,0:T(8,128)S(1)} %get-tuple-element.78), channel_id=1, source_target_pairs={{0,8},{8,0},{16,24},{24,16},{32,40},{40,32},{48,56},{56,48},{64,72... | collective-permute-start | bytes 49160 | tf_op jit(solution)/shard_map/ppermute | solution.py:481
  30.7 5.9 %collective-permute-start.12 = (f32[32,2048]{1,0:T(8,128)S(1)}, f32[32,2048]{1,0:T(8,128)S(1)}, u32[]{:S(2)}, u32[]{:S(2)}) collective-permute-start(f32[32,2048]{1,0:T(8,128)S(1)} %get-tuple-element.81), channel_id=1, source_target_pairs={{1,2},{3,4},{5,6},{9,10},{11,12},{13,14},{17,18},{19,20},{21,22},{... | collective-permute-start | bytes 786440 | tf_op jit(solution)/shard_map/ppermute | solution.py:479
  32.3 4.3 %collective-permute-start.15 = (f32[32,2048]{1,0:T(8,128)S(1)}, f32[32,2048]{1,0:T(8,128)S(1)}, u32[]{:S(2)}, u32[]{:S(2)}) collective-permute-start(f32[32,2048]{1,0:T(8,128)S(1)} %get-tuple-element.84), channel_id=1, source_target_pairs={{0,1},{1,0},{2,3},{3,2},{4,5},{5,4},{6,7},{7,6},{8,9},{9,8},{10,11... | collective-permute-start | bytes 786440 | tf_op jit(solution)/shard_map/ppermute | solution.py:482
  32.3 3.7 %collective-permute-start.14 = (f32[32,128]{1,0:T(8,128)S(1)}, f32[32,128]{1,0:T(8,128)S(1)}, u32[]{:S(2)}, u32[]{:S(2)}) collective-permute-start(f32[32,128]{1,0:T(8,128)S(1)} %get-tuple-element.83), channel_id=1, source_target_pairs={{0,8},{8,0},{16,24},{24,16},{32,40},{40,32},{48,56},{56,48},{64,72... | collective-permute-start | bytes 49160 | tf_op jit(solution)/shard_map/ppermute | solution.py:481
  33.2 2.9 %collective-permute-start.13 = (f32[32,128]{1,0:T(8,128)S(1)}, f32[32,128]{1,0:T(8,128)S(1)}, u32[]{:S(2)}, u32[]{:S(2)}) collective-permute-start(f32[32,128]{1,0:T(8,128)S(1)} %get-tuple-element.82.after), channel_id=1, source_target_pairs={{8,16},{9,17},{10,18},{11,19},{12,20},{13,21},{14,22},{15,23},{24,... | collective-permute-start | bytes 49160 | tf_op jit(solution)/shard_map/ppermute | solution.py:480
  37.4 8.1 %collective-permute-start.16 = (f32[32,2048]{1,0:T(8,128)S(1)}, f32[32,2048]{1,0:T(8,128)S(1)}, u32[]{:S(2)}, u32[]{:S(2)}) collective-permute-start(f32[32,2048]{1,0:T(8,128)S(1)} %get-tuple-element.87), channel_id=1, source_target_pairs={{1,2},{3,4},{5,6},{9,10},{11,12},{13,14},{17,18},{19,20},{21,22},{... | collective-permute-start | bytes 786440 | tf_op jit(solution)/shard_map/ppermute | solution.py:479
  41.2 4.3 %collective-permute-start.19 = (f32[32,2048]{1,0:T(8,128)S(1)}, f32[32,2048]{1,0:T(8,128)S(1)}, u32[]{:S(2)}, u32[]{:S(2)}) collective-permute-start(f32[32,2048]{1,0:T(8,128)S(1)} %get-tuple-element.90), channel_id=1, source_target_pairs={{0,1},{1,0},{2,3},{3,2},{4,5},{5,4},{6,7},{7,6},{8,9},{9,8},{10,11... | collective-permute-start | bytes 786440 | tf_op jit(solution)/shard_map/ppermute | solution.py:482
  41.2 2.0 %collective-permute-start.17 = (f32[32,128]{1,0:T(8,128)S(1)}, f32[32,128]{1,0:T(8,128)S(1)}, u32[]{:S(2)}, u32[]{:S(2)}) collective-permute-start(f32[32,128]{1,0:T(8,128)S(1)} %get-tuple-element.88), channel_id=1, source_target_pairs={{8,16},{9,17},{10,18},{11,19},{12,20},{13,21},{14,22},{15,23},{24,... | collective-permute-start | bytes 49160 | tf_op jit(solution)/shard_map/ppermute | solution.py:480
  41.7 3.7 %collective-permute-start.18 = (f32[32,128]{1,0:T(8,128)S(1)}, f32[32,128]{1,0:T(8,128)S(1)}, u32[]{:S(2)}, u32[]{:S(2)}) collective-permute-start(f32[32,128]{1,0:T(8,128)S(1)} %get-tuple-element.89), channel_id=1, source_target_pairs={{0,8},{8,0},{16,24},{24,16},{32,40},{40,32},{48,56},{56,48},{64,72... | collective-permute-start | bytes 49160 | tf_op jit(solution)/shard_map/ppermute | solution.py:481
  46.3 6.9 %collective-permute-start.20 = (f32[32,2048]{1,0:T(8,128)S(1)}, f32[32,2048]{1,0:T(8,128)S(1)}, u32[]{:S(2)}, u32[]{:S(2)}) collective-permute-start(f32[32,2048]{1,0:T(8,128)S(1)} %get-tuple-element.92), channel_id=1, source_target_pairs={{1,2},{3,4},{5,6},{9,10},{11,12},{13,14},{17,18},{19,20},{21,22},{... | collective-permute-start | bytes 786440 | tf_op jit(solution)/shard_map/ppermute | solution.py:479
  48.9 4.3 %collective-permute-start.23 = (f32[32,2048]{1,0:T(8,128)S(1)}, f32[32,2048]{1,0:T(8,128)S(1)}, u32[]{:S(2)}, u32[]{:S(2)}) collective-permute-start(f32[32,2048]{1,0:T(8,128)S(1)} %get-tuple-element.95), channel_id=1, source_target_pairs={{0,1},{1,0},{2,3},{3,2},{4,5},{5,4},{6,7},{7,6},{8,9},{9,8},{10,11... | collective-permute-start | bytes 786440 | tf_op jit(solution)/shard_map/ppermute | solution.py:482
  48.9 1.7 %collective-permute-start.21 = (f32[32,128]{1,0:T(8,128)S(1)}, f32[32,128]{1,0:T(8,128)S(1)}, u32[]{:S(2)}, u32[]{:S(2)}) collective-permute-start(f32[32,128]{1,0:T(8,128)S(1)} %get-tuple-element.93), channel_id=1, source_target_pairs={{8,16},{9,17},{10,18},{11,19},{12,20},{13,21},{14,22},{15,23},{24,... | collective-permute-start | bytes 49160 | tf_op jit(solution)/shard_map/ppermute | solution.py:480
  49.5 3.7 %collective-permute-start.22 = (f32[32,128]{1,0:T(8,128)S(1)}, f32[32,128]{1,0:T(8,128)S(1)}, u32[]{:S(2)}, u32[]{:S(2)}) collective-permute-start(f32[32,128]{1,0:T(8,128)S(1)} %get-tuple-element.94), channel_id=1, source_target_pairs={{0,8},{8,0},{16,24},{24,16},{32,40},{40,32},{48,56},{56,48},{64,72... | collective-permute-start | bytes 49160 | tf_op jit(solution)/shard_map/ppermute | solution.py:481
  53.9 7.2 %collective-permute-start.24 = (f32[32,2048]{1,0:T(8,128)S(1)}, f32[32,2048]{1,0:T(8,128)S(1)}, u32[]{:S(2)}, u32[]{:S(2)}) collective-permute-start(f32[32,2048]{1,0:T(8,128)S(1)} %get-tuple-element.97), channel_id=1, source_target_pairs={{1,2},{3,4},{5,6},{9,10},{11,12},{13,14},{17,18},{19,20},{21,22},{... | collective-permute-start | bytes 786440 | tf_op jit(solution)/shard_map/ppermute | solution.py:479
  56.9 4.3 %collective-permute-start.27 = (f32[32,2048]{1,0:T(8,128)S(1)}, f32[32,2048]{1,0:T(8,128)S(1)}, u32[]{:S(2)}, u32[]{:S(2)}) collective-permute-start(f32[32,2048]{1,0:T(8,128)S(1)} %get-tuple-element.100), channel_id=1, source_target_pairs={{0,1},{1,0},{2,3},{3,2},{4,5},{5,4},{6,7},{7,6},{8,9},{9,8},{10,11... | collective-permute-start | bytes 786440 | tf_op jit(solution)/shard_map/ppermute | solution.py:482
  56.9 1.7 %collective-permute-start.25 = (f32[32,128]{1,0:T(8,128)S(1)}, f32[32,128]{1,0:T(8,128)S(1)}, u32[]{:S(2)}, u32[]{:S(2)}) collective-permute-start(f32[32,128]{1,0:T(8,128)S(1)} %get-tuple-element.98), channel_id=1, source_target_pairs={{8,16},{9,17},{10,18},{11,19},{12,20},{13,21},{14,22},{15,23},{24,... | collective-permute-start | bytes 49160 | tf_op jit(solution)/shard_map/ppermute | solution.py:480
  57.4 3.7 %collective-permute-start.26 = (f32[32,128]{1,0:T(8,128)S(1)}, f32[32,128]{1,0:T(8,128)S(1)}, u32[]{:S(2)}, u32[]{:S(2)}) collective-permute-start(f32[32,128]{1,0:T(8,128)S(1)} %get-tuple-element.99), channel_id=1, source_target_pairs={{0,8},{8,0},{16,24},{24,16},{32,40},{40,32},{48,56},{56,48},{64,72... | collective-permute-start | bytes 49160 | tf_op jit(solution)/shard_map/ppermute | solution.py:481
  61.8 7.7 %collective-permute-start.28 = (f32[32,2048]{1,0:T(8,128)S(1)}, f32[32,2048]{1,0:T(8,128)S(1)}, u32[]{:S(2)}, u32[]{:S(2)}) collective-permute-start(f32[32,2048]{1,0:T(8,128)S(1)} %get-tuple-element.102), channel_id=1, source_target_pairs={{1,2},{3,4},{5,6},{9,10},{11,12},{13,14},{17,18},{19,20},{21,22},{... | collective-permute-start | bytes 786440 | tf_op jit(solution)/shard_map/ppermute | solution.py:479
  65.2 4.4 %collective-permute-start.31 = (f32[32,2048]{1,0:T(8,128)S(1)}, f32[32,2048]{1,0:T(8,128)S(1)}, u32[]{:S(2)}, u32[]{:S(2)}) collective-permute-start(f32[32,2048]{1,0:T(8,128)S(1)} %get-tuple-element.105), channel_id=1, source_target_pairs={{0,1},{1,0},{2,3},{3,2},{4,5},{5,4},{6,7},{7,6},{8,9},{9,8},{10,11... | collective-permute-start | bytes 786440 | tf_op jit(solution)/shard_map/ppermute | solution.py:482
  65.2 4.4 %collective-permute-start.29 = (f32[32,128]{1,0:T(8,128)S(1)}, f32[32,128]{1,0:T(8,128)S(1)}, u32[]{:S(2)}, u32[]{:S(2)}) collective-permute-start(f32[32,128]{1,0:T(8,128)S(1)} %get-tuple-element.103), channel_id=1, source_target_pairs={{8,16},{9,17},{10,18},{11,19},{12,20},{13,21},{14,22},{15,23},{24,... | collective-permute-start | bytes 49160 | tf_op jit(solution)/shard_map/ppermute | solution.py:480
  65.7 3.9 %collective-permute-start.30 = (f32[32,128]{1,0:T(8,128)S(1)}, f32[32,128]{1,0:T(8,128)S(1)}, u32[]{:S(2)}, u32[]{:S(2)}) collective-permute-start(f32[32,128]{1,0:T(8,128)S(1)} %get-tuple-element.104), channel_id=1, source_target_pairs={{0,8},{8,0},{16,24},{24,16},{32,40},{40,32},{48,56},{56,48},{64,72... | collective-permute-start | bytes 49160 | tf_op jit(solution)/shard_map/ppermute | solution.py:481
where the time goes:
time: 95.1 us; the launch traced here: 93.9 us
  starting transfers between devices  38.5 us (40%)
  Pallas kernels  22.8 us (24%)
  blocking collectives  18.5 us (19%)
  waiting for transfers between devices  11.4 us (12%)
  local copies, waits for them, and re-layouts  1.87 us (2%)
    all_to_all x1, blocking collectives, local(): shares = lax.all_to_all(parts, 'gx', 0, 0, tiled=True)  18.5 us
    ppermute x8, starting transfers between devices, exchange(): ze = lax.ppermute(ze, ('gx', 'gz'), z_far)  18.1 us
    ppermute x8, starting transfers between devices, exchange(): xe = lax.ppermute(xe, 'gx', x_even)  15.2 us
    ppermute x8, waiting for transfers between devices, exchange(): xe = lax.ppermute(xe, 'gx', x_even)  10.8 us
    pallas_call x7, Pallas kernels, half_sweep(): pl.pallas_call(functools.partial(relax_kernel, colour), in_specs=[vmem()]...  5.33 us
    pallas_call x1, Pallas kernels, last_half_sweep(): pl.pallas_call(functools.partial(last_kernel, scale), in_specs=[vmem()] *...  4.58 us
    pallas_call x1, Pallas kernels, pack(): pl.pallas_call(pack_kernel, in_specs=[hbm()] * 3, out_specs=[vmem()] * 8,...  4.26 us
    pallas_call x1, Pallas kernels, pack_charge(): pl.pallas_call(charge_kernel, in_specs=[hbm(), vmem(), vmem(), anywhere()...  2.99 us
  transfers between devices with their start and end apart: 32, of which 7 were waited for; matrix products, arithmetic and copies ran while one was open for 0% of the time, Pallas kernels for 9%

commit v1 on v0

--- a/solution.py
+++ b/solution.py
@@ -18,7 +18,8 @@
 PITCH = 9
 PINNED = 1e30
 VMEM_BYTES = 16 * 1024 * 1024
-PACK_VMEM_BYTES = 50 * 1024 * 1024
+PACK_VMEM_BYTES = 51 * 1024 * 1024
+REST_VMEM_BYTES = 46 * 1024 * 1024
 
 
 def vmem():
@@ -93,51 +94,71 @@
                 sides(*z_refs, *x_refs)
 
 
-def spread_rows(source, tiles, even):
-    for j in range(tiles):
+def spread_rows(source, tiles, even, wanted):
+    for j in wanted:
         a = source[pl.ds(2 * j, 8, stride=2 * tiles), :]
         b = source[pl.ds(2 * j + 1, 8, stride=2 * tiles), :]
         yield pl.ds(8 * j, 8), jnp.where(even, a, b), jnp.where(even, b, a)
 
 
-def pack_kernel(pot_hbm, reg_hbm, lev_hbm, f0_ref, f1_ref, m0_ref, m1_ref, ze_ref, xo_ref, xe_ref, zi_ref, lev_ref,
-                pot_ref, reg_ref, field, mark, lev_sem, sems):
-    planes, rows, columns = f0_ref.shape
-    lev_copy = pltpu.make_async_copy(lev_hbm, lev_ref, lev_sem)
-    lev_copy.start()
-    copies = [
-        [
-            pltpu.make_async_copy(source.at[z], target.at[z], sems.at[z, i])
-            for i, (source, target) in enumerate(((reg_hbm, reg_ref), (pot_hbm, pot_ref)))
-        ]
-        for z in range(planes)
-    ]
-    for plane in copies:
-        for copy in plane:
-            copy.start()
-    lev_copy.wait()
+def level_table(lev_ref):
     lane = lax.broadcasted_iota(jnp.int32, (8, LANES), 1)
     table = jnp.zeros((8, LANES), jnp.float32)
     for region in range(1, lev_ref.shape[0]):
         table = jnp.where(lane == region, lev_ref[region], table)
-    for z in range(planes):
+    return table
+
+
+def start_field(table, reg_ref, pot_ref, z, j, at):
+    region = reg_ref[z, pl.ds(j, 8), at]
+    pinned = jnp.take_along_axis(table, region, axis=1)
+    free = region == 0
+    return jnp.where(free, pot_ref[z, pl.ds(j, 8), at], pinned), jnp.where(free, 0.0, PINNED)
+
+
+def pack_kernel(pot_hbm, reg_hbm, lev_hbm, f0_ref, f1_ref, m0_ref, m1_ref, ze_ref, xo_ref, xe_ref, zi_ref, lev_ref,
+                pot_ref, reg_ref, field, mark, one, lev_sem, sems):
+    planes, rows, columns = one.shape
+    tiles = rows // 8
+    lev_copy = pltpu.make_async_copy(lev_hbm, lev_ref, lev_sem)
+    lev_copy.start()
+    parts = {z: ((0, 2 * rows),) if z in (0, planes - 1) else ((0, 8), (2 * rows - 8, 8)) for z in range(planes)}
+    order = sorted(parts, key=lambda z: len(parts[z]))
+    copies = {
+        z: [
+            pltpu.make_async_copy(source.at[z, pl.ds(j, size)], target.at[z, pl.ds(j, size)], sems.at[z, i, k])
+            for k, (j, size) in enumerate(parts[z])
+            for i, (source, target) in enumerate(((reg_hbm, reg_ref), (pot_hbm, pot_ref)))
+        ]
+        for z in order
+    }
+    for z in order:
+        for copy in copies[z]:
+            copy.start()
+    lev_copy.wait()
+    table = level_table(lev_ref)
+    for z in order:
         even = column_parity(8, LANES) == z % 2
         for copy in copies[z]:
             copy.wait()
+        whole = z in (0, planes - 1)
         for c, at in chunks(columns):
             slot = z % 2 * (columns // LANES) + c
-            for j in range(0, 2 * rows, 8):
-                to = pl.ds(j, 8)
-                region = reg_ref[z, to, at]
-                pinned = jnp.take_along_axis(table, region, axis=1)
-                free = region == 0
-                field[slot, to, :] = jnp.where(free, pot_ref[z, to, at], pinned)
-                mark[slot, to, :] = jnp.where(free, 0.0, PINNED)
-            for source, out0, out1 in ((field, f0_ref, f1_ref), (mark, m0_ref, m1_ref)):
-                for to, a, b in spread_rows(source.at[slot], rows // 8, even):
-                    out0[z, to, at] = a
-                    out1[z, to, at] = b
-    sends(f1_ref, 1, *position()[:2], ze_ref, xo_ref, xe_ref, zi_ref)
+            for first, size in parts[z]:
+                for j in range(first, first + size, 8):
+                    field[slot, pl.ds(j, 8), :], mark[slot, pl.ds(j, 8), :] = start_field(
+                        table, reg_ref, pot_ref, z, j, at
+                    )
+            for to, a, b in spread_rows(field.at[slot], tiles, even, range(tiles) if whole else (0, tiles - 1)):
+                one[z, to, at] = b
+                if whole:
+                    f0_ref[z // (planes - 1), to, at] = a
+                    f1_ref[z // (planes - 1), to, at] = b
+            if whole:
+                for to, a, b in spread_rows(mark.at[slot], tiles, even, range(tiles)):
+                    m0_ref[z // (planes - 1), to, at] = a
+                    m1_ref[z // (planes - 1), to, at] = b
+    sends(one, 1, *position()[:2], ze_ref, xo_ref, xe_ref, zi_ref)
 
 
 def send_shapes(planes, rows, columns):
@@ -154,15 +175,16 @@
         pack_kernel,
         in_specs=[hbm()] * 3,
         out_specs=[vmem()] * 8,
-        out_shape=[half] * 4 + send_shapes(*half.shape),
+        out_shape=[shape_of(2, *half.shape[1:])] * 4 + send_shapes(*half.shape),
         scratch_shapes=[
             pltpu.SMEM(levels.shape, jnp.float32),
             pltpu.VMEM(whole, jnp.float32),
             pltpu.VMEM(whole, jnp.int32),
             stage,
             stage,
+            pltpu.VMEM(half.shape, jnp.float32),
             pltpu.SemaphoreType.DMA,
-            pltpu.SemaphoreType.DMA((planes, 2)),
+            pltpu.SemaphoreType.DMA((planes, 2, 2)),
         ],
         compiler_params=pltpu.CompilerParams(vmem_limit_bytes=PACK_VMEM_BYTES),
         cost_estimate=cost(20 * potential.size, 8 * potential.size),
@@ -170,42 +192,75 @@
     )(potential, regions, levels)
 
 
-def charge_kernel(chg_hbm, m0_ref, m1_ref, after, c0_ref, c1_ref, done_ref, chg_ref, stage, sems):
+def rest_kernel(pot_hbm, reg_hbm, chg_hbm, lev_hbm, f0_ref, f1_ref, m0_ref, m1_ref, after, zero_ref, one_ref, c0_ref,
+                c1_ref, done_ref, lev_ref, pot_ref, reg_ref, chg_ref, field, stage, lev_sem, sems):
     del after
     done_ref[...] = jnp.zeros_like(done_ref)
-    planes, rows, columns = m0_ref.shape
-    copies = [pltpu.make_async_copy(chg_hbm.at[z], chg_ref.at[z], sems.at[z]) for z in range(planes)]
-    for copy in copies:
-        copy.start()
-    for z in range(planes):
+    planes, rows, columns = zero_ref.shape
+    tiles = rows // 8
+    lev_copy = pltpu.make_async_copy(lev_hbm, lev_ref, lev_sem)
+    lev_copy.start()
+    inner = range(1, planes - 1)
+    order = [*inner, 0, planes - 1]
+    copies = {}
+    for z in order:
+        pairs = ((reg_hbm, reg_ref), (pot_hbm, pot_ref), (chg_hbm, chg_ref))
+        copies[z] = [
+            pltpu.make_async_copy(source.at[z], target.at[z], sems.at[z, i])
+            for i, (source, target) in enumerate(pairs)
+            if z in inner or i == 2
+        ]
+        for copy in copies[z]:
+            copy.start()
+    lev_copy.wait()
+    table = level_table(lev_ref)
+    for z in (0, planes - 1):
+        zero_ref[z] = f0_ref[z // (planes - 1)]
+        one_ref[z] = f1_ref[z // (planes - 1)]
+    for z in order:
         even = column_parity(8, LANES) == z % 2
-        copies[z].wait()
+        for copy in copies[z]:
+            copy.wait()
         for c, at in chunks(columns):
             slot = z % 2 * (columns // LANES) + c
             for j in range(0, 2 * rows, 8):
-                stage[slot, pl.ds(j, 8), :] = chg_ref[z, pl.ds(j, 8), at]
-            for to, a, b in spread_rows(stage.at[slot], rows // 8, even):
-                c0_ref[z, to, at] = m0_ref[z, to, at] + a
-                c1_ref[z, to, at] = m1_ref[z, to, at] + b
-
-
-def pack_charge(charge, marks, after):
+                charge = chg_ref[z, pl.ds(j, 8), at]
+                if z in inner:
+                    field[slot, pl.ds(j, 8), :], mark = start_field(table, reg_ref, pot_ref, z, j, at)
+                    charge = charge + mark
+                stage[slot, pl.ds(j, 8), :] = charge
+            for to, a, b in spread_rows(stage.at[slot], tiles, even, range(tiles)):
+                c0_ref[z, to, at] = a if z in inner else m0_ref[z // (planes - 1), to, at] + a
+                c1_ref[z, to, at] = b if z in inner else m1_ref[z // (planes - 1), to, at] + b
+            if z in inner:
+                for to, a, b in spread_rows(field.at[slot], tiles, even, range(tiles)):
+                    zero_ref[z, to, at] = a
+                    one_ref[z, to, at] = b
+
+
+def pack_rest(potential, regions, charge, levels, packed, after):
     planes, rows, columns = charge.shape
     half = shape_of(planes, rows // 2, columns)
+    stage = pltpu.VMEM((2 * columns // LANES, rows, LANES), jnp.float32)
     return pl.pallas_call(
-        charge_kernel,
-        in_specs=[hbm(), vmem(), vmem(), anywhere()],
-        out_specs=[vmem()] * 3,
-        out_shape=[half, half, shape_of(8, LANES)],
+        rest_kernel,
+        in_specs=[hbm()] * 4 + [vmem()] * 4 + [anywhere()],
+        out_specs=[vmem()] * 5,
+        out_shape=[half] * 4 + [shape_of(8, LANES)],
         scratch_shapes=[
+            pltpu.SMEM(levels.shape, jnp.float32),
             pltpu.VMEM(charge.shape, jnp.float32),
-            pltpu.VMEM((2 * columns // LANES, rows, LANES), jnp.float32),
-            pltpu.SemaphoreType.DMA((planes,)),
+            pltpu.VMEM(charge.shape, jnp.int32),
+            pltpu.VMEM(charge.shape, jnp.float32),
+            stage,
+            stage,
+            pltpu.SemaphoreType.DMA,
+            pltpu.SemaphoreType.DMA((planes, 3)),
         ],
-        compiler_params=pltpu.CompilerParams(vmem_limit_bytes=PACK_VMEM_BYTES),
-        cost_estimate=cost(20 * charge.size, 4 * charge.size),
-        name="charge",
-    )(charge, *marks, after)
+        compiler_params=pltpu.CompilerParams(vmem_limit_bytes=REST_VMEM_BYTES),
+        cost_estimate=cost(40 * charge.size, 8 * charge.size),
+        name="pack_rest",
+    )(potential, regions, charge, levels, *packed, after)
 
 
 def relax(own_ref, other_ref, charge_ref, ze_ref, xo_ref, xe_ref, zi_ref, below, above, colour, put):
@@ -219,35 +274,36 @@
     below[...] = jnp.where(below_live, jnp.where(odd == 0, xo, xe), 0.0)
     above[...] = jnp.where(above_live, jnp.where(odd == 0, xe, xo), 0.0)
 
-    for z in range(planes):
+    def tile_step(z, j):
         first_row = parity == (z + colour) % 2
-        for j in range(tiles):
-            rows_at = pl.ds(8 * j, 8)
-            for c, at in chunks(columns):
-                tile = lambda t, at=at: other_ref[z, pl.ds(8 * t, 8), at]
-                mid = tile(j)
-                if z in (0, planes - 1):
-                    far = jnp.where(far_live, ze_ref[rows_at, at], 0.0)
-                    near = zi_ref[rows_at, at]
-                z_low = other_ref[z - 1, rows_at, at] if z else jnp.where(core == 0, far, near)
-                z_high = other_ref[z + 1, rows_at, at] if z < planes - 1 else jnp.where(core == 0, near, far)
-                line = pl.ds(z // 2 * count + c, 1)
-                if j:
-                    x_low = tile(j - 1)
-                else:
-                    x_low = jnp.where(row == 0, below[line, :], pltpu.roll(tile(tiles - 1), 1, 0))
-                if j < tiles - 1:
-                    x_high = tile(j + 1)
-                else:
-                    x_high = jnp.where(row == 7, above[line, :], pltpu.roll(tile(0), 7, 0))
-                left = other_ref[z, rows_at, pl.ds(LANES * (c - 1), LANES)] if c else 0.0
-                right = other_ref[z, rows_at, pl.ds(LANES * (c + 1), LANES)] if c < count - 1 else 0.0
-                y_low = pltpu.roll(jnp.where(lane == LANES - 1, left, mid), 1, 1)
-                y_high = pltpu.roll(jnp.where(lane == 0, right, mid), LANES - 1, 1)
-                charge = charge_ref[z, rows_at, at]
-                beside = z_low + z_high + mid + jnp.where(first_row, x_low, x_high) + y_low + y_high
-                own = own_ref[z, rows_at, at]
-                put(z, j, c, jnp.where(charge < PINNED, 0.25 * (beside + charge) - 0.5 * own, own))
+        rows_at = pl.ds(8 * j, 8)
+        for c, at in chunks(columns):
+            tile = lambda t, at=at: other_ref[z, pl.ds(8 * t, 8), at]
+            mid = tile(j)
+            if z in (0, planes - 1):
+                far = jnp.where(far_live, ze_ref[rows_at, at], 0.0)
+                near = zi_ref[rows_at, at]
+            z_low = other_ref[z - 1, rows_at, at] if z else jnp.where(core == 0, far, near)
+            z_high = other_ref[z + 1, rows_at, at] if z < planes - 1 else jnp.where(core == 0, near, far)
+            line = pl.ds(z // 2 * count + c, 1)
+            if j:
+                x_low = tile(j - 1)
+            else:
+                x_low = jnp.where(row == 0, below[line, :], pltpu.roll(tile(tiles - 1), 1, 0))
+            if j < tiles - 1:
+                x_high = tile(j + 1)
+            else:
+                x_high = jnp.where(row == 7, above[line, :], pltpu.roll(tile(0), 7, 0))
+            left = other_ref[z, rows_at, pl.ds(LANES * (c - 1), LANES)] if c else 0.0
+            right = other_ref[z, rows_at, pl.ds(LANES * (c + 1), LANES)] if c < count - 1 else 0.0
+            y_low = pltpu.roll(jnp.where(lane == LANES - 1, left, mid), 1, 1)
+            y_high = pltpu.roll(jnp.where(lane == 0, right, mid), LANES - 1, 1)
+            charge = charge_ref[z, rows_at, at]
+            beside = z_low + z_high + mid + jnp.where(first_row, x_low, x_high) + y_low + y_high
+            own = own_ref[z, rows_at, at]
+            put(z, j, c, jnp.where(charge < PINNED, 0.25 * (beside + charge) - 0.5 * own, own))
+
+    return tile_step
 
 
 def line_scratch(planes, columns):
@@ -261,7 +317,10 @@
     def put(z, j, c, value):
         out_ref[z, pl.ds(8 * j, 8), pl.ds(LANES * c, LANES)] = value
 
-    relax(own_ref, other_ref, charge_ref, ze_ref, xo_ref, xe_ref, zi_ref, below, above, colour, put)
+    step = relax(own_ref, other_ref, charge_ref, ze_ref, xo_ref, xe_ref, zi_ref, below, above, colour, put)
+    for z in range(own_ref.shape[0]):
+        for j in range(own_ref.shape[1] // 8):
+            step(z, j)
     sends(out_ref, colour, *position()[:2], ze_out, xo_out, xe_out, zi_out)
 
 
@@ -338,36 +397,42 @@
     pairs = planes // 2
     n, m = 16 * TURNS, 16 * STEPS * pairs
     tiles = tables[0][0].shape[0]
-    for e in (0, 1):
+    totals = [None, None]
+
+    def add_tile(e, j):
         left_ref, radial_ref = tables[e]
-        total = None
-        for j in range(tiles):
-            slot = (e * tiles + j) % right.shape[0]
+        slot = (e * tiles + j) % right.shape[0]
+        for k in range(pairs):
+            f = field_of(2 * k + (e + colour) % 2, j)
+            twice = jnp.concatenate([f, f], axis=0)
+            for b in range(0, 2 * STEPS, 2):
+                high, low = split(twice * radial_ref[j, pl.ds(8 * b, 16), :])
+                index = 2 * STEPS * k + b
+                right[slot, pl.ds(8 * index, 16), :] = high
+                right[slot, pl.ds(m + 8 * index, 16), :] = low
+        product = jnp.dot(right[slot], left_ref[j], preferred_element_type=jnp.float32)
+        totals[e] = product if totals[e] is None else totals[e] + product
+
+    def finish():
+        for e in (0, 1):
+            total = totals[e]
+            total = ((total[:m, :n] + total[m:, :n]) + (total[:m, n:] + total[m:, n:])).T
+            i = lax.broadcasted_iota(jnp.int32, total.shape, 0)
+            k = lax.broadcasted_iota(jnp.int32, total.shape, 1)
+            total = jnp.sum(jnp.where(i % 8 == k % 8, total, 0.0).reshape(2 * TURNS, 8, m), axis=1)
+            for shift in (1, 2, 4):
+                total = total + pltpu.roll(total, shift, 1)
+            half = 8 * STEPS
+            even, odd = total[:TURNS], total[TURNS:]
+            cosines = even - pltpu.roll(odd, m - half, 1)
+            sines = odd + pltpu.roll(even, m - half, 1)
+            lane = lax.broadcasted_iota(jnp.int32, (TURNS, m), 1)
+            total = jnp.where(lane // half % 2 == 0, cosines, pltpu.roll(sines, half, 1))
             for k in range(pairs):
-                f = field_of(2 * k + (e + colour) % 2, j)
-                twice = jnp.concatenate([f, f], axis=0)
-                for b in range(0, 2 * STEPS, 2):
-                    high, low = split(twice * radial_ref[j, pl.ds(8 * b, 16), :])
-                    index = 2 * STEPS * k + b
-                    right[slot, pl.ds(8 * index, 16), :] = high
-                    right[slot, pl.ds(m + 8 * index, 16), :] = low
-            product = jnp.dot(right[slot], left_ref[j], preferred_element_type=jnp.float32)
-            total = product if total is None else total + product
-        total = ((total[:m, :n] + total[m:, :n]) + (total[:m, n:] + total[m:, n:])).T
-        i = lax.broadcasted_iota(jnp.int32, total.shape, 0)
-        k = lax.broadcasted_iota(jnp.int32, total.shape, 1)
-        total = jnp.sum(jnp.where(i % 8 == k % 8, total, 0.0).reshape(2 * TURNS, 8, m), axis=1)
-        for shift in (1, 2, 4):
-            total = total + pltpu.roll(total, shift, 1)
-        half = 8 * STEPS
-        even, odd = total[:TURNS], total[TURNS:]
-        cosines = even - pltpu.roll(odd, m - half, 1)
-        sines = odd + pltpu.roll(even, m - half, 1)
-        lane = lax.broadcasted_iota(jnp.int32, (TURNS, m), 1)
-        total = jnp.where(lane // half % 2 == 0, cosines, pltpu.roll(sines, half, 1))
-        for k in range(pairs):
-            outs[2 * k + (e + colour) % 2] = total[:, 2 * half * k : 2 * half * (k + 1)]
-    return jnp.concatenate(outs, axis=1)
+                outs[2 * k + (e + colour) % 2] = total[:, 2 * half * k : 2 * half * (k + 1)]
+        return jnp.concatenate(outs, axis=1)
+
+    return add_tile, finish
 
 
 def right_scratch(planes, columns):
@@ -380,13 +445,14 @@
 
 def multipole_kernel(field_ref, left0, radial0, left1, radial1, out_ref, done_ref, right):
     done_ref[...] = jnp.zeros_like(done_ref)
-    out_ref[...] = multipoles_of(
-        0,
-        lambda z, j: field_ref[z, pl.ds(8 * j, 8), :],
-        ((left0, radial0), (left1, radial1)),
-        field_ref.shape[0],
-        right,
+    planes, rows, _ = field_ref.shape
+    add_tile, finish = multipoles_of(
+        0, lambda z, j: field_ref[z, pl.ds(8 * j, 8), :], ((left0, radial0), (left1, radial1)), planes, right
     )
+    for e in (0, 1):
+        for j in range(rows // 8):
+            add_tile(e, j)
+    out_ref[...] = finish()
 
 
 def multipole_sums(field, tables):
@@ -422,11 +488,20 @@
             copy.start()
             copies.append(copy)
 
-    relax(own_ref, other_ref, charge_ref, ze_ref, xo_ref, xe_ref, zi_ref, below, above, 1, put)
-    sums = multipoles_of(
+    relax_tile = relax(own_ref, other_ref, charge_ref, ze_ref, xo_ref, xe_ref, zi_ref, below, above, 1, put)
+    add_tile, finish = multipoles_of(
         1, lambda z, j: one[z, pl.ds(8 * j, 8), :], ((left0, radial0), (left1, radial1)), planes, right
     )
-    out_ref[...] = (sums + sums_ref[...]) * scale
+    for z in range(1, planes, 2):
+        for j in range(tiles):
+            relax_tile(z, j)
+    for j in range(tiles):
+        add_tile(0, j)
+        for z in range(0, planes, 2):
+            relax_tile(z, j)
+    for j in range(tiles):
+        add_tile(1, j)
+    out_ref[...] = (finish() + sums_ref[...]) * scale
     for copy in copies:
         copy.wait()
 
@@ -482,9 +557,9 @@
         zi = lax.ppermute(zi, "gz", z_near)
         return ze, xo, xe, zi
 
-    zero, one, *rest = pack(potential, regions, levels)
-    marks, out = rest[:2], rest[2:]
-    charge0, charge1, after = pack_charge(charge, marks, out[1])
+    *packed, ze, xo, xe, zi = pack(potential, regions, levels)
+    out = ze, xo, xe, zi
+    zero, one, charge0, charge1, after = pack_rest(potential, regions, charge, levels, packed, xo)
     tables = []
     for sweep in range(SWEEPS):
         halos = exchange(*out)

time: 95.1 us -> 93.3 us (0.981)
  Pallas kernels: 22.8 us -> 20.9 us
    pallas_call x1, Pallas kernels: 4.26 us -> 2.81 us  [pack(): pl.pallas_call(pack_kernel, in_specs=[hbm()] * 3, out_specs=[vmem()] * 8,...]
where the time goes in v1:
time: 93.3 us; the launch traced here: 92.2 us
  starting transfers between devices  38.6 us (41%)
  Pallas kernels  20.9 us (22%)
  blocking collectives  18.5 us (20%)
  waiting for transfers between devices  11.4 us (12%)
  local copies, waits for them, and re-layouts  1.87 us (2%)
    all_to_all x1, blocking collectives, local(): shares = lax.all_to_all(parts, 'gx', 0, 0, tiled=True)  18.5 us
    ppermute x8, starting transfers between devices, exchange(): ze = lax.ppermute(ze, ('gx', 'gz'), z_far)  18.3 us
    ppermute x8, starting transfers between devices, exchange(): xe = lax.ppermute(xe, 'gx', x_even)  15.2 us
    ppermute x8, waiting for transfers between devices, exchange(): xe = lax.ppermute(xe, 'gx', x_even)  10.8 us
    pallas_call x7, Pallas kernels, half_sweep(): pl.pallas_call(functools.partial(relax_kernel, colour), in_specs=[vmem()]...  5.34 us
    pallas_call x1, Pallas kernels, last_half_sweep(): pl.pallas_call(functools.partial(last_kernel, scale), in_specs=[vmem()] *...  4.31 us
    pallas_call x1, Pallas kernels, multipole_sums(): pl.pallas_call(multipole_kernel, in_specs=[vmem()] * 5, out_specs=[vmem()...  2.9 us
    pallas_call x1, Pallas kernels, pack(): pl.pallas_call(pack_kernel, in_specs=[hbm()] * 3, out_specs=[vmem()] * 8,...  2.81 us
  transfers between devices with their start and end apart: 32, of which 7 were waited for; matrix products, arithmetic and copies ran while one was open for 0% of the time, Pallas kernels for 9%

profile of v1, /device:TPU:8, one launch (start us, length us, event | category | flops | bytes accessed | tf_op | source)
XLA Modules:
  0.0 92.2 jit_solution(14071336884745490095)
XLA Ops:
  0.6 0.6 copy-done
  1.3 2.8 %pack.1 = (f32[2,32,2048]{2,1,0:T(8,128)S(1)}, f32[2,32,2048]{2,1,0:T(8,128)S(1)}, f32[2,32,2048]{2,1,0:T(8,128)S(1)}, f32[2,32,2048]{2,1,0:T(8,128)S(1)}, f32[3...) custom-call(f32[4,64,2048]{2,1,0:T(8,128)} %pot_hbm.3, ...), custom_call_target="tpu_custom_call" | custom-call | flops 10485760 | bytes 4194304 | tf_op jit(solution)/shard_map/pack/pallas_call | solution.py:174
  4.1 0.1 collective-permute-start
  4.2 1.7 %collective-permute-start.3 = (f32[32,2048]{1,0:T(8,128)S(1)}, f32[32,2048]{1,0:T(8,128)S(1)}, u32[]{:S(2)}, u32[]{:S(2)}) collective-permute-start(f32[32,2048]{1,0:T(8,128)S(1)} %get-tuple-element.70), channel_id=1, source_target_pairs={{0,1},{1,0},{2,3},{3,2},{4,5},{5,4},{6,7},{7,6},{8,9},{9,8},{10,11... | collective-permute-start | bytes 786440 | tf_op jit(solution)/shard_map/ppermute | solution.py:557
  5.9 1.9 %collective-permute-start.2 = (f32[32,128]{1,0:T(8,128)S(1)}, f32[32,128]{1,0:T(8,128)S(1)}, u32[]{:S(2)}, u32[]{:S(2)}) collective-permute-start(f32[32,128]{1,0:T(8,128)S(1)} %get-tuple-element.69), channel_id=1, source_target_pairs={{0,8},{8,0},{16,24},{24,16},{32,40},{40,32},{48,56},{56,48},{64,72... | collective-permute-start | bytes 49160 | tf_op jit(solution)/shard_map/ppermute | solution.py:556
  7.8 2.8 %pack_rest.1 = (f32[4,32,2048]{2,1,0:T(8,128)S(1)}, f32[4,32,2048]{2,1,0:T(8,128)S(1)}, f32[4,32,2048]{2,1,0:T(8,128)S(1)}, f32[4,32,2048]{2,1,0:T(8,128)S(1)}, f32[8,128]{1,0:T(8,128)S(1)}) custom-call(f32[4,64,2048]{2,1,0:T(8,128)} %pot_hbm.3, s32[4,64,2048]{2,1,0:T(8,128)} %reg_hbm.3, f32[4,64,2048]{2,1,0:T(8,128)} %chg_hbm.1, f32[16]{0:T(128)S(1)} %copy-done.1, ...), custom_call_target="tpu_custom_call" | custom-call | flops 20971520 | bytes 4194304 | tf_op jit(solution)/shard_map/pack_rest/pallas_call | solution.py:245
  10.6 0.7 relax.7
  11.4 0.6 collective-permute-start.4
  12.0 0.8 collective-permute-start.7
  12.9 3.8 %collective-permute-start.6 = (f32[32,128]{1,0:T(8,128)S(1)}, f32[32,128]{1,0:T(8,128)S(1)}, u32[]{:S(2)}, u32[]{:S(2)}) collective-permute-start(f32[32,128]{1,0:T(8,128)S(1)} %get-tuple-element.76), channel_id=1, source_target_pairs={{0,8},{8,0},{16,24},{24,16},{32,40},{40,32},{48,56},{56,48},{64,72... | collective-permute-start | bytes 49160 | tf_op jit(solution)/shard_map/ppermute | solution.py:556
  16.7 1.4 %angles.2 = (bf16[4,2048,256]{2,1,0:T(8,128)(2,1)S(1)}, f32[4,64,2048]{2,1,0:T(8,128)S(1)}, f32[8,128]{1,0:T(8,128)S(1)}) custom-call(f32[32,128]{1,0:T(8,128)S(1)} %get-tuple-element.75.after), custom_call_target="tpu_custom_call" | custom-call | flops 8388608 | tf_op jit(solution)/shard_map/angles/pallas_call | solution.py:383
  18.1 0.3 collective-permute-done.6.xe_ref
  18.4 0.8 relax.8
  19.2 3.0 %collective-permute-start.8 = (f32[32,2048]{1,0:T(8,128)S(1)}, f32[32,2048]{1,0:T(8,128)S(1)}, u32[]{:S(2)}, u32[]{:S(2)}) collective-permute-start(f32[32,2048]{1,0:T(8,128)S(1)} %get-tuple-element.80), channel_id=1, source_target_pairs={{1,2},{3,4},{5,6},{9,10},{11,12},{13,14},{17,18},{19,20},{21,22},{... | collective-permute-start | bytes 786440 | tf_op jit(solution)/shard_map/ppermute | solution.py:554
  22.2 0.5 collective-permute-start.9
  22.7 3.8 %collective-permute-start.10 = (f32[32,128]{1,0:T(8,128)S(1)}, f32[32,128]{1,0:T(8,128)S(1)}, u32[]{:S(2)}, u32[]{:S(2)}) collective-permute-start(f32[32,128]{1,0:T(8,128)S(1)} %get-tuple-element.82), channel_id=1, source_target_pairs={{0,8},{8,0},{16,24},{24,16},{32,40},{40,32},{48,56},{56,48},{64,72... | collective-permute-start | bytes 49160 | tf_op jit(solution)/shard_map/ppermute | solution.py:556
  26.5 1.7 %collective-permute-done.10.xe_ref = f32[32,128]{1,0:T(8,128)S(1)} collective-permute-done((f32[32,128]{1,0:T(8,128)S(1)}, f32[32,128]{1,0:T(8,128)S(1)}, u32[]{:S(2)}, u32[]{:S(2)}) %collective-permute-start.10) | collective-permute-done | bytes 16416 | tf_op jit(solution)/shard_map/ppermute | solution.py:556
  28.2 0.8 relax.9
  29.1 1.6 %collective-permute-start.12 = (f32[32,2048]{1,0:T(8,128)S(1)}, f32[32,2048]{1,0:T(8,128)S(1)}, u32[]{:S(2)}, u32[]{:S(2)}) collective-permute-start(f32[32,2048]{1,0:T(8,128)S(1)} %get-tuple-element.85), channel_id=1, source_target_pairs={{1,2},{3,4},{5,6},{9,10},{11,12},{13,14},{17,18},{19,20},{21,22},{... | collective-permute-start | bytes 786440 | tf_op jit(solution)/shard_map/ppermute | solution.py:554
  30.7 0.8 collective-permute-start.14
  31.6 1.4 %angles.3 = (bf16[4,2048,256]{2,1,0:T(8,128)(2,1)S(1)}, f32[4,64,2048]{2,1,0:T(8,128)S(1)}, f32[8,128]{1,0:T(8,128)S(1)}) custom-call(f32[32,128]{1,0:T(8,128)S(1)} %get-tuple-element.86.after), custom_call_target="tpu_custom_call" | custom-call | flops 8388608 | tf_op jit(solution)/shard_map/angles/pallas_call | solution.py:383
  33.0 1.5 %collective-permute-done.14.xe_ref = f32[32,128]{1,0:T(8,128)S(1)} collective-permute-done((f32[32,128]{1,0:T(8,128)S(1)}, f32[32,128]{1,0:T(8,128)S(1)}, u32[]{:S(2)}, u32[]{:S(2)}) %collective-permute-start.14) | collective-permute-done | bytes 16416 | tf_op jit(solution)/shard_map/ppermute | solution.py:556
  34.4 0.5 collective-permute-done.12.ze_ref
  34.9 0.7 relax.10
  35.7 4.0 %collective-permute-start.16 = (f32[32,2048]{1,0:T(8,128)S(1)}, f32[32,2048]{1,0:T(8,128)S(1)}, u32[]{:S(2)}, u32[]{:S(2)}) collective-permute-start(f32[32,2048]{1,0:T(8,128)S(1)} %get-tuple-element.91), channel_id=1, source_target_pairs={{1,2},{3,4},{5,6},{9,10},{11,12},{13,14},{17,18},{19,20},{21,22},{... | collective-permute-start | bytes 786440 | tf_op jit(solution)/shard_map/ppermute | solution.py:554
  39.7 0.5 collective-permute-start.17
  40.2 1.5 %collective-permute-start.18 = (f32[32,128]{1,0:T(8,128)S(1)}, f32[32,128]{1,0:T(8,128)S(1)}, u32[]{:S(2)}, u32[]{:S(2)}) collective-permute-start(f32[32,128]{1,0:T(8,128)S(1)} %get-tuple-element.93), channel_id=1, source_target_pairs={{0,8},{8,0},{16,24},{24,16},{32,40},{40,32},{48,56},{56,48},{64,72... | collective-permute-start | bytes 49160 | tf_op jit(solution)/shard_map/ppermute | solution.py:556
  41.7 2.2 %collective-permute-done.18.xe_ref = f32[32,128]{1,0:T(8,128)S(1)} collective-permute-done((f32[32,128]{1,0:T(8,128)S(1)}, f32[32,128]{1,0:T(8,128)S(1)}, u32[]{:S(2)}, u32[]{:S(2)}) %collective-permute-start.18) | collective-permute-done | bytes 16416 | tf_op jit(solution)/shard_map/ppermute | solution.py:556
  44.0 0.8 relax.11
  44.7 2.7 %collective-permute-start.20 = (f32[32,2048]{1,0:T(8,128)S(1)}, f32[32,2048]{1,0:T(8,128)S(1)}, u32[]{:S(2)}, u32[]{:S(2)}) collective-permute-start(f32[32,2048]{1,0:T(8,128)S(1)} %get-tuple-element.96), channel_id=1, source_target_pairs={{1,2},{3,4},{5,6},{9,10},{11,12},{13,14},{17,18},{19,20},{21,22},{... | collective-permute-start | bytes 786440 | tf_op jit(solution)/shard_map/ppermute | solution.py:554
  47.4 0.5 collective-permute-start.21
  47.9 1.1 %collective-permute-start.22 = (f32[32,128]{1,0:T(8,128)S(1)}, f32[32,128]{1,0:T(8,128)S(1)}, u32[]{:S(2)}, u32[]{:S(2)}) collective-permute-start(f32[32,128]{1,0:T(8,128)S(1)} %get-tuple-element.98), channel_id=1, source_target_pairs={{0,8},{8,0},{16,24},{24,16},{32,40},{40,32},{48,56},{56,48},{64,72... | collective-permute-start | bytes 49160 | tf_op jit(solution)/shard_map/ppermute | solution.py:556
  49.1 2.6 %collective-permute-done.22.xe_ref = f32[32,128]{1,0:T(8,128)S(1)} collective-permute-done((f32[32,128]{1,0:T(8,128)S(1)}, f32[32,128]{1,0:T(8,128)S(1)}, u32[]{:S(2)}, u32[]{:S(2)}) %collective-permute-start.22) | collective-permute-done | bytes 16416 | tf_op jit(solution)/shard_map/ppermute | solution.py:556
  51.7 0.8 relax.12
  52.4 2.9 %collective-permute-start.24 = (f32[32,2048]{1,0:T(8,128)S(1)}, f32[32,2048]{1,0:T(8,128)S(1)}, u32[]{:S(2)}, u32[]{:S(2)}) collective-permute-start(f32[32,2048]{1,0:T(8,128)S(1)} %get-tuple-element.101), channel_id=1, source_target_pairs={{1,2},{3,4},{5,6},{9,10},{11,12},{13,14},{17,18},{19,20},{21,22},{... | collective-permute-start | bytes 786440 | tf_op jit(solution)/shard_map/ppermute | solution.py:554
  55.4 0.5 collective-permute-start.25
  55.9 1.2 %collective-permute-start.26 = (f32[32,128]{1,0:T(8,128)S(1)}, f32[32,128]{1,0:T(8,128)S(1)}, u32[]{:S(2)}, u32[]{:S(2)}) collective-permute-start(f32[32,128]{1,0:T(8,128)S(1)} %get-tuple-element.103), channel_id=1, source_target_pairs={{0,8},{8,0},{16,24},{24,16},{32,40},{40,32},{48,56},{56,48},{64,72... | collective-permute-start | bytes 49160 | tf_op jit(solution)/shard_map/ppermute | solution.py:556
  57.1 2.5 %collective-permute-done.26.xe_ref = f32[32,128]{1,0:T(8,128)S(1)} collective-permute-done((f32[32,128]{1,0:T(8,128)S(1)}, f32[32,128]{1,0:T(8,128)S(1)}, u32[]{:S(2)}, u32[]{:S(2)}) %collective-permute-start.26) | collective-permute-done | bytes 16416 | tf_op jit(solution)/shard_map/ppermute | solution.py:556
  59.6 0.7 relax.13
  60.4 3.3 %collective-permute-start.28 = (f32[32,2048]{1,0:T(8,128)S(1)}, f32[32,2048]{1,0:T(8,128)S(1)}, u32[]{:S(2)}, u32[]{:S(2)}) collective-permute-start(f32[32,2048]{1,0:T(8,128)S(1)} %get-tuple-element.106), channel_id=1, source_target_pairs={{1,2},{3,4},{5,6},{9,10},{11,12},{13,14},{17,18},{19,20},{21,22},{... | collective-permute-start | bytes 786440 | tf_op jit(solution)/shard_map/ppermute | solution.py:554
  63.7 0.5 collective-permute-start.29
  64.2 0.9 %collective-permute-start.30 = (f32[32,128]{1,0:T(8,128)S(1)}, f32[32,128]{1,0:T(8,128)S(1)}, u32[]{:S(2)}, u32[]{:S(2)}) collective-permute-start(f32[32,128]{1,0:T(8,128)S(1)} %get-tuple-element.108), channel_id=1, source_target_pairs={{0,8},{8,0},{16,24},{24,16},{32,40},{40,32},{48,56},{56,48},{64,72... | collective-permute-start | bytes 49160 | tf_op jit(solution)/shard_map/ppermute | solution.py:556
  65.2 2.9 %multipole.1 = (f32[8,256]{1,0:T(8,128)S(1)}, f32[8,128]{1,0:T(8,128)S(1)}) custom-call(f32[4,32,2048]{2,1,0:T(8,128)S(1)} %get-tuple-element.105.field_ref.other_ref, bf16[4,2048,256]{2,1,0:T(8,128)(2,1)S(1)} %get-tuple-element.110.left0, f32[4,64,2048]{2,1,0:T(8,128)S(1)} %get-tuple-element.111.radial0, ...), custom_call_target="tpu_custom_call" | custom-call | flops 26214400 | tf_op jit(solution)/shard_map/multipole/pallas_call | solution.py:460
  68.1 4.3 %relax_last.1 = (f32[4,64,2048]{2,1,0:T(8,128)}, f32[8,256]{1,0:T(8,128)S(1)}) custom-call(f32[4,32,2048]{2,1,0:T(8,128)S(1)} %get-tuple-element.100.other_ref.after.own_ref, f32[4,32,2048]{2,1,0:T(8,128)S(1)} %get-tuple-element.105.field_ref.other_ref, f32[4,32,2048]{2,1,0:T(8,128)S(1)} %get-tuple-element.73.charge_ref, ...), custom_call_target="tpu_custom_call" | custom-call | flops 26214400 | tf_op jit(solution)/shard_map/relax_last/pallas_call | solution.py:511
  72.4 0.1 slice.3
  72.6 0.1 copy.12
  72.9 18.5 %all_to_all.9 = f32[32,1,8]{2,1,0:T(1,128)S(1)} all-to-all(f32[32,1,8]{2,1,0:T(1,128)S(1)} %copy.14), channel_id=1, replica_groups=mesh['gx'=32,'gz'=8] {'gx'}, dimensions={0} | all-to-all | bytes 2048 | tf_op jit(solution)/shard_map/all_to_all | solution.py:581
  91.6 0.7 copy.15
  (42 shorter events, 0.6 us)
Async XLA Ops:
  0.6 0.7 copy-start
  1.3 6.5 %copy-start.1 = (f32[16]{0:T(128)S(1)}, f32[16]{0:T(128)}, u32[]{:S(2)}) copy-start(f32[16]{0:T(128)} %lev_hbm.3) | copy-start | bytes 196
  4.1 6.5 %collective-permute-start = (f32[32,2048]{1,0:T(8,128)S(1)}, f32[32,2048]{1,0:T(8,128)S(1)}, u32[]{:S(2)}, u32[]{:S(2)}) collective-permute-start(f32[32,2048]{1,0:T(8,128)S(1)} %get-tuple-element.68), channel_id=1, source_target_pairs={{1,2},{3,4},{5,6},{9,10},{11,12},{13,14},{17,18},{19,20},{21,22},{... | collective-permute-start | bytes 786440 | tf_op jit(solution)/shard_map/ppermute | solution.py:554
  4.2 6.4 %collective-permute-start.3 = (f32[32,2048]{1,0:T(8,128)S(1)}, f32[32,2048]{1,0:T(8,128)S(1)}, u32[]{:S(2)}, u32[]{:S(2)}) collective-permute-start(f32[32,2048]{1,0:T(8,128)S(1)} %get-tuple-element.70), channel_id=1, source_target_pairs={{0,1},{1,0},{2,3},{3,2},{4,5},{5,4},{6,7},{7,6},{8,9},{9,8},{10,11... | collective-permute-start | bytes 786440 | tf_op jit(solution)/shard_map/ppermute | solution.py:557
  5.9 4.7 %collective-permute-start.2 = (f32[32,128]{1,0:T(8,128)S(1)}, f32[32,128]{1,0:T(8,128)S(1)}, u32[]{:S(2)}, u32[]{:S(2)}) collective-permute-start(f32[32,128]{1,0:T(8,128)S(1)} %get-tuple-element.69), channel_id=1, source_target_pairs={{0,8},{8,0},{16,24},{24,16},{32,40},{40,32},{48,56},{56,48},{64,72... | collective-permute-start | bytes 49160 | tf_op jit(solution)/shard_map/ppermute | solution.py:556
  7.8 2.8 %collective-permute-start.1 = (f32[32,128]{1,0:T(8,128)S(1)}, f32[32,128]{1,0:T(8,128)S(1)}, u32[]{:S(2)}, u32[]{:S(2)}) collective-permute-start(f32[32,128]{1,0:T(8,128)S(1)} %get-tuple-element.64.after), channel_id=1, source_target_pairs={{8,16},{9,17},{10,18},{11,19},{12,20},{13,21},{14,22},{15,23},{24,... | collective-permute-start | bytes 49160 | tf_op jit(solution)/shard_map/ppermute | solution.py:555
  11.4 7.0 %collective-permute-start.4 = (f32[32,2048]{1,0:T(8,128)S(1)}, f32[32,2048]{1,0:T(8,128)S(1)}, u32[]{:S(2)}, u32[]{:S(2)}) collective-permute-start(f32[32,2048]{1,0:T(8,128)S(1)} %get-tuple-element.74), channel_id=1, source_target_pairs={{1,2},{3,4},{5,6},{9,10},{11,12},{13,14},{17,18},{19,20},{21,22},{... | collective-permute-start | bytes 786440 | tf_op jit(solution)/shard_map/ppermute | solution.py:554
  12.0 6.4 %collective-permute-start.7 = (f32[32,2048]{1,0:T(8,128)S(1)}, f32[32,2048]{1,0:T(8,128)S(1)}, u32[]{:S(2)}, u32[]{:S(2)}) collective-permute-start(f32[32,2048]{1,0:T(8,128)S(1)} %get-tuple-element.77), channel_id=1, source_target_pairs={{0,1},{1,0},{2,3},{3,2},{4,5},{5,4},{6,7},{7,6},{8,9},{9,8},{10,11... | collective-permute-start | bytes 786440 | tf_op jit(solution)/shard_map/ppermute | solution.py:557
  12.9 5.5 %collective-permute-start.6 = (f32[32,128]{1,0:T(8,128)S(1)}, f32[32,128]{1,0:T(8,128)S(1)}, u32[]{:S(2)}, u32[]{:S(2)}) collective-permute-start(f32[32,128]{1,0:T(8,128)S(1)} %get-tuple-element.76), channel_id=1, source_target_pairs={{0,8},{8,0},{16,24},{24,16},{32,40},{40,32},{48,56},{56,48},{64,72... | collective-permute-start | bytes 49160 | tf_op jit(solution)/shard_map/ppermute | solution.py:556
  16.7 1.7 %collective-permute-start.5 = (f32[32,128]{1,0:T(8,128)S(1)}, f32[32,128]{1,0:T(8,128)S(1)}, u32[]{:S(2)}, u32[]{:S(2)}) collective-permute-start(f32[32,128]{1,0:T(8,128)S(1)} %get-tuple-element.75.after), channel_id=1, source_target_pairs={{8,16},{9,17},{10,18},{11,19},{12,20},{13,21},{14,22},{15,23},{24,... | collective-permute-start | bytes 49160 | tf_op jit(solution)/shard_map/ppermute | solution.py:555
  19.2 9.0 %collective-permute-start.8 = (f32[32,2048]{1,0:T(8,128)S(1)}, f32[32,2048]{1,0:T(8,128)S(1)}, u32[]{:S(2)}, u32[]{:S(2)}) collective-permute-start(f32[32,2048]{1,0:T(8,128)S(1)} %get-tuple-element.80), channel_id=1, source_target_pairs={{1,2},{3,4},{5,6},{9,10},{11,12},{13,14},{17,18},{19,20},{21,22},{... | collective-permute-start | bytes 786440 | tf_op jit(solution)/shard_map/ppermute | solution.py:554
  22.2 6.0 %collective-permute-start.11 = (f32[32,2048]{1,0:T(8,128)S(1)}, f32[32,2048]{1,0:T(8,128)S(1)}, u32[]{:S(2)}, u32[]{:S(2)}) collective-permute-start(f32[32,2048]{1,0:T(8,128)S(1)} %get-tuple-element.83), channel_id=1, source_target_pairs={{0,1},{1,0},{2,3},{3,2},{4,5},{5,4},{6,7},{7,6},{8,9},{9,8},{10,11... | collective-permute-start | bytes 786440 | tf_op jit(solution)/shard_map/ppermute | solution.py:557
  22.2 4.3 %collective-permute-start.9 = (f32[32,128]{1,0:T(8,128)S(1)}, f32[32,128]{1,0:T(8,128)S(1)}, u32[]{:S(2)}, u32[]{:S(2)}) collective-permute-start(f32[32,128]{1,0:T(8,128)S(1)} %get-tuple-element.81), channel_id=1, source_target_pairs={{8,16},{9,17},{10,18},{11,19},{12,20},{13,21},{14,22},{15,23},{24,... | collective-permute-start | bytes 49160 | tf_op jit(solution)/shard_map/ppermute | solution.py:555
  22.7 5.5 %collective-permute-start.10 = (f32[32,128]{1,0:T(8,128)S(1)}, f32[32,128]{1,0:T(8,128)S(1)}, u32[]{:S(2)}, u32[]{:S(2)}) collective-permute-start(f32[32,128]{1,0:T(8,128)S(1)} %get-tuple-element.82), channel_id=1, source_target_pairs={{0,8},{8,0},{16,24},{24,16},{32,40},{40,32},{48,56},{56,48},{64,72... | collective-permute-start | bytes 49160 | tf_op jit(solution)/shard_map/ppermute | solution.py:556
  29.1 5.9 %collective-permute-start.12 = (f32[32,2048]{1,0:T(8,128)S(1)}, f32[32,2048]{1,0:T(8,128)S(1)}, u32[]{:S(2)}, u32[]{:S(2)}) collective-permute-start(f32[32,2048]{1,0:T(8,128)S(1)} %get-tuple-element.85), channel_id=1, source_target_pairs={{1,2},{3,4},{5,6},{9,10},{11,12},{13,14},{17,18},{19,20},{21,22},{... | collective-permute-start | bytes 786440 | tf_op jit(solution)/shard_map/ppermute | solution.py:554
  30.7 4.3 %collective-permute-start.15 = (f32[32,2048]{1,0:T(8,128)S(1)}, f32[32,2048]{1,0:T(8,128)S(1)}, u32[]{:S(2)}, u32[]{:S(2)}) collective-permute-start(f32[32,2048]{1,0:T(8,128)S(1)} %get-tuple-element.88), channel_id=1, source_target_pairs={{0,1},{1,0},{2,3},{3,2},{4,5},{5,4},{6,7},{7,6},{8,9},{9,8},{10,11... | collective-permute-start | bytes 786440 | tf_op jit(solution)/shard_map/ppermute | solution.py:557
  30.7 3.7 %collective-permute-start.14 = (f32[32,128]{1,0:T(8,128)S(1)}, f32[32,128]{1,0:T(8,128)S(1)}, u32[]{:S(2)}, u32[]{:S(2)}) collective-permute-start(f32[32,128]{1,0:T(8,128)S(1)} %get-tuple-element.87), channel_id=1, source_target_pairs={{0,8},{8,0},{16,24},{24,16},{32,40},{40,32},{48,56},{56,48},{64,72... | collective-permute-start | bytes 49160 | tf_op jit(solution)/shard_map/ppermute | solution.py:556
  31.5 2.9 %collective-permute-start.13 = (f32[32,128]{1,0:T(8,128)S(1)}, f32[32,128]{1,0:T(8,128)S(1)}, u32[]{:S(2)}, u32[]{:S(2)}) collective-permute-start(f32[32,128]{1,0:T(8,128)S(1)} %get-tuple-element.86.after), channel_id=1, source_target_pairs={{8,16},{9,17},{10,18},{11,19},{12,20},{13,21},{14,22},{15,23},{24,... | collective-permute-start | bytes 49160 | tf_op jit(solution)/shard_map/ppermute | solution.py:555
  35.7 8.3 %collective-permute-start.16 = (f32[32,2048]{1,0:T(8,128)S(1)}, f32[32,2048]{1,0:T(8,128)S(1)}, u32[]{:S(2)}, u32[]{:S(2)}) collective-permute-start(f32[32,2048]{1,0:T(8,128)S(1)} %get-tuple-element.91), channel_id=1, source_target_pairs={{1,2},{3,4},{5,6},{9,10},{11,12},{13,14},{17,18},{19,20},{21,22},{... | collective-permute-start | bytes 786440 | tf_op jit(solution)/shard_map/ppermute | solution.py:554
  39.7 4.3 %collective-permute-start.19 = (f32[32,2048]{1,0:T(8,128)S(1)}, f32[32,2048]{1,0:T(8,128)S(1)}, u32[]{:S(2)}, u32[]{:S(2)}) collective-permute-start(f32[32,2048]{1,0:T(8,128)S(1)} %get-tuple-element.94), channel_id=1, source_target_pairs={{0,1},{1,0},{2,3},{3,2},{4,5},{5,4},{6,7},{7,6},{8,9},{9,8},{10,11... | collective-permute-start | bytes 786440 | tf_op jit(solution)/shard_map/ppermute | solution.py:557
  39.7 2.0 %collective-permute-start.17 = (f32[32,128]{1,0:T(8,128)S(1)}, f32[32,128]{1,0:T(8,128)S(1)}, u32[]{:S(2)}, u32[]{:S(2)}) collective-permute-start(f32[32,128]{1,0:T(8,128)S(1)} %get-tuple-element.92), channel_id=1, source_target_pairs={{8,16},{9,17},{10,18},{11,19},{12,20},{13,21},{14,22},{15,23},{24,... | collective-permute-start | bytes 49160 | tf_op jit(solution)/shard_map/ppermute | solution.py:555
  40.2 3.7 %collective-permute-start.18 = (f32[32,128]{1,0:T(8,128)S(1)}, f32[32,128]{1,0:T(8,128)S(1)}, u32[]{:S(2)}, u32[]{:S(2)}) collective-permute-start(f32[32,128]{1,0:T(8,128)S(1)} %get-tuple-element.93), channel_id=1, source_target_pairs={{0,8},{8,0},{16,24},{24,16},{32,40},{40,32},{48,56},{56,48},{64,72... | collective-permute-start | bytes 49160 | tf_op jit(solution)/shard_map/ppermute | solution.py:556
  44.7 6.9 %collective-permute-start.20 = (f32[32,2048]{1,0:T(8,128)S(1)}, f32[32,2048]{1,0:T(8,128)S(1)}, u32[]{:S(2)}, u32[]{:S(2)}) collective-permute-start(f32[32,2048]{1,0:T(8,128)S(1)} %get-tuple-element.96), channel_id=1, source_target_pairs={{1,2},{3,4},{5,6},{9,10},{11,12},{13,14},{17,18},{19,20},{21,22},{... | collective-permute-start | bytes 786440 | tf_op jit(solution)/shard_map/ppermute | solution.py:554
  47.4 4.3 %collective-permute-start.23 = (f32[32,2048]{1,0:T(8,128)S(1)}, f32[32,2048]{1,0:T(8,128)S(1)}, u32[]{:S(2)}, u32[]{:S(2)}) collective-permute-start(f32[32,2048]{1,0:T(8,128)S(1)} %get-tuple-element.99), channel_id=1, source_target_pairs={{0,1},{1,0},{2,3},{3,2},{4,5},{5,4},{6,7},{7,6},{8,9},{9,8},{10,11... | collective-permute-start | bytes 786440 | tf_op jit(solution)/shard_map/ppermute | solution.py:557
  47.4 1.7 %collective-permute-start.21 = (f32[32,128]{1,0:T(8,128)S(1)}, f32[32,128]{1,0:T(8,128)S(1)}, u32[]{:S(2)}, u32[]{:S(2)}) collective-permute-start(f32[32,128]{1,0:T(8,128)S(1)} %get-tuple-element.97), channel_id=1, source_target_pairs={{8,16},{9,17},{10,18},{11,19},{12,20},{13,21},{14,22},{15,23},{24,... | collective-permute-start | bytes 49160 | tf_op jit(solution)/shard_map/ppermute | solution.py:555
  47.9 3.7 %collective-permute-start.22 = (f32[32,128]{1,0:T(8,128)S(1)}, f32[32,128]{1,0:T(8,128)S(1)}, u32[]{:S(2)}, u32[]{:S(2)}) collective-permute-start(f32[32,128]{1,0:T(8,128)S(1)} %get-tuple-element.98), channel_id=1, source_target_pairs={{0,8},{8,0},{16,24},{24,16},{32,40},{40,32},{48,56},{56,48},{64,72... | collective-permute-start | bytes 49160 | tf_op jit(solution)/shard_map/ppermute | solution.py:556
  52.4 7.2 %collective-permute-start.24 = (f32[32,2048]{1,0:T(8,128)S(1)}, f32[32,2048]{1,0:T(8,128)S(1)}, u32[]{:S(2)}, u32[]{:S(2)}) collective-permute-start(f32[32,2048]{1,0:T(8,128)S(1)} %get-tuple-element.101), channel_id=1, source_target_pairs={{1,2},{3,4},{5,6},{9,10},{11,12},{13,14},{17,18},{19,20},{21,22},{... | collective-permute-start | bytes 786440 | tf_op jit(solution)/shard_map/ppermute | solution.py:554
  55.4 4.3 %collective-permute-start.27 = (f32[32,2048]{1,0:T(8,128)S(1)}, f32[32,2048]{1,0:T(8,128)S(1)}, u32[]{:S(2)}, u32[]{:S(2)}) collective-permute-start(f32[32,2048]{1,0:T(8,128)S(1)} %get-tuple-element.104), channel_id=1, source_target_pairs={{0,1},{1,0},{2,3},{3,2},{4,5},{5,4},{6,7},{7,6},{8,9},{9,8},{10,11... | collective-permute-start | bytes 786440 | tf_op jit(solution)/shard_map/ppermute | solution.py:557
  55.4 1.7 %collective-permute-start.25 = (f32[32,128]{1,0:T(8,128)S(1)}, f32[32,128]{1,0:T(8,128)S(1)}, u32[]{:S(2)}, u32[]{:S(2)}) collective-permute-start(f32[32,128]{1,0:T(8,128)S(1)} %get-tuple-element.102), channel_id=1, source_target_pairs={{8,16},{9,17},{10,18},{11,19},{12,20},{13,21},{14,22},{15,23},{24,... | collective-permute-start | bytes 49160 | tf_op jit(solution)/shard_map/ppermute | solution.py:555
  55.9 3.7 %collective-permute-start.26 = (f32[32,128]{1,0:T(8,128)S(1)}, f32[32,128]{1,0:T(8,128)S(1)}, u32[]{:S(2)}, u32[]{:S(2)}) collective-permute-start(f32[32,128]{1,0:T(8,128)S(1)} %get-tuple-element.103), channel_id=1, source_target_pairs={{0,8},{8,0},{16,24},{24,16},{32,40},{40,32},{48,56},{56,48},{64,72... | collective-permute-start | bytes 49160 | tf_op jit(solution)/shard_map/ppermute | solution.py:556
  60.4 7.7 %collective-permute-start.28 = (f32[32,2048]{1,0:T(8,128)S(1)}, f32[32,2048]{1,0:T(8,128)S(1)}, u32[]{:S(2)}, u32[]{:S(2)}) collective-permute-start(f32[32,2048]{1,0:T(8,128)S(1)} %get-tuple-element.106), channel_id=1, source_target_pairs={{1,2},{3,4},{5,6},{9,10},{11,12},{13,14},{17,18},{19,20},{21,22},{... | collective-permute-start | bytes 786440 | tf_op jit(solution)/shard_map/ppermute | solution.py:554
  63.7 4.4 %collective-permute-start.31 = (f32[32,2048]{1,0:T(8,128)S(1)}, f32[32,2048]{1,0:T(8,128)S(1)}, u32[]{:S(2)}, u32[]{:S(2)}) collective-permute-start(f32[32,2048]{1,0:T(8,128)S(1)} %get-tuple-element.109), channel_id=1, source_target_pairs={{0,1},{1,0},{2,3},{3,2},{4,5},{5,4},{6,7},{7,6},{8,9},{9,8},{10,11... | collective-permute-start | bytes 786440 | tf_op jit(solution)/shard_map/ppermute | solution.py:557
  63.7 4.4 %collective-permute-start.29 = (f32[32,128]{1,0:T(8,128)S(1)}, f32[32,128]{1,0:T(8,128)S(1)}, u32[]{:S(2)}, u32[]{:S(2)}) collective-permute-start(f32[32,128]{1,0:T(8,128)S(1)} %get-tuple-element.107), channel_id=1, source_target_pairs={{8,16},{9,17},{10,18},{11,19},{12,20},{13,21},{14,22},{15,23},{24,... | collective-permute-start | bytes 49160 | tf_op jit(solution)/shard_map/ppermute | solution.py:555
  64.2 3.9 %collective-permute-start.30 = (f32[32,128]{1,0:T(8,128)S(1)}, f32[32,128]{1,0:T(8,128)S(1)}, u32[]{:S(2)}, u32[]{:S(2)}) collective-permute-start(f32[32,128]{1,0:T(8,128)S(1)} %get-tuple-element.108), channel_id=1, source_target_pairs={{0,8},{8,0},{16,24},{24,16},{32,40},{40,32},{48,56},{56,48},{64,72... | collective-permute-start | bytes 49160 | tf_op jit(solution)/shard_map/ppermute | solution.py:556

commit v2 on v1

--- a/solution.py
+++ b/solution.py
@@ -576,10 +576,9 @@
     scale = 1.0 / math.sqrt(rows_total * columns)
     field, sums = last_half_sweep(one, zero, charge1, halos, tables, sums, after, scale)
     share = K // nx
-    parts = jnp.transpose(sums[:, 7::8].reshape(TURNS, planes, 2, STEPS), (1, 2, 0, 3)).reshape(planes, nx, share)
-    parts = jnp.transpose(parts, (1, 0, 2)).reshape(nx, planes * share)
+    parts = jnp.transpose(sums[:, 7::8].reshape(TURNS, planes, 2, STEPS), (2, 0, 3, 1)).reshape(nx, share * planes)
     shares = lax.all_to_all(parts, "gx", 0, 0, tiled=True)
-    return field, jnp.sum(shares, axis=0).reshape(planes, share)
+    return field, jnp.sum(shares, axis=0).reshape(share, planes).T
 
 
 def solution(mesh):

time: 93.3 us -> 93.1 us (level)
  no operation moved by 1% of the time
where the time goes in v2:
time: 93.1 us; the launch traced here: 92 us
  starting transfers between devices  38.6 us (41%)
  Pallas kernels  20.9 us (22%)
  blocking collectives  18.5 us (20%)
  waiting for transfers between devices  11.4 us (12%)
  local copies, waits for them, and re-layouts  1.69 us (2%)
    all_to_all x1, blocking collectives, local(): shares = lax.all_to_all(parts, 'gx', 0, 0, tiled=True)  18.5 us
    ppermute x8, starting transfers between devices, exchange(): ze = lax.ppermute(ze, ('gx', 'gz'), z_far)  18.3 us
    ppermute x8, starting transfers between devices, exchange(): xe = lax.ppermute(xe, 'gx', x_even)  15.2 us
    ppermute x8, waiting for transfers between devices, exchange(): xe = lax.ppermute(xe, 'gx', x_even)  10.8 us
    pallas_call x7, Pallas kernels, half_sweep(): pl.pallas_call(functools.partial(relax_kernel, colour), in_specs=[vmem()]...  5.34 us
    pallas_call x1, Pallas kernels, last_half_sweep(): pl.pallas_call(functools.partial(last_kernel, scale), in_specs=[vmem()] *...  4.31 us
    pallas_call x1, Pallas kernels, multipole_sums(): pl.pallas_call(multipole_kernel, in_specs=[vmem()] * 5, out_specs=[vmem()...  2.9 us
    pallas_call x1, Pallas kernels, pack(): pl.pallas_call(pack_kernel, in_specs=[hbm()] * 3, out_specs=[vmem()] * 8,...  2.81 us
  transfers between devices with their start and end apart: 32, of which 7 were waited for; matrix products, arithmetic and copies ran while one was open for 0% of the time, Pallas kernels for 9%

profile of v2, /device:TPU:8, one launch (start us, length us, event | category | flops | bytes accessed | tf_op | source)
XLA Modules:
  0.0 92.0 jit_solution(13287014447610639218)
XLA Ops:
  0.6 0.6 copy-done
  1.3 2.8 %pack.1 = (f32[2,32,2048]{2,1,0:T(8,128)S(1)}, f32[2,32,2048]{2,1,0:T(8,128)S(1)}, f32[2,32,2048]{2,1,0:T(8,128)S(1)}, f32[2,32,2048]{2,1,0:T(8,128)S(1)}, f32[3...) custom-call(f32[4,64,2048]{2,1,0:T(8,128)} %pot_hbm.3, ...), custom_call_target="tpu_custom_call" | custom-call | flops 10485760 | bytes 4194304 | tf_op jit(solution)/shard_map/pack/pallas_call | solution.py:174
  4.1 0.1 collective-permute-start
  4.2 1.7 %collective-permute-start.3 = (f32[32,2048]{1,0:T(8,128)S(1)}, f32[32,2048]{1,0:T(8,128)S(1)}, u32[]{:S(2)}, u32[]{:S(2)}) collective-permute-start(f32[32,2048]{1,0:T(8,128)S(1)} %get-tuple-element.70), channel_id=1, source_target_pairs={{0,1},{1,0},{2,3},{3,2},{4,5},{5,4},{6,7},{7,6},{8,9},{9,8},{10,11... | collective-permute-start | bytes 786440 | tf_op jit(solution)/shard_map/ppermute | solution.py:557
  5.9 1.9 %collective-permute-start.2 = (f32[32,128]{1,0:T(8,128)S(1)}, f32[32,128]{1,0:T(8,128)S(1)}, u32[]{:S(2)}, u32[]{:S(2)}) collective-permute-start(f32[32,128]{1,0:T(8,128)S(1)} %get-tuple-element.69), channel_id=1, source_target_pairs={{0,8},{8,0},{16,24},{24,16},{32,40},{40,32},{48,56},{56,48},{64,72... | collective-permute-start | bytes 49160 | tf_op jit(solution)/shard_map/ppermute | solution.py:556
  7.8 2.8 %pack_rest.1 = (f32[4,32,2048]{2,1,0:T(8,128)S(1)}, f32[4,32,2048]{2,1,0:T(8,128)S(1)}, f32[4,32,2048]{2,1,0:T(8,128)S(1)}, f32[4,32,2048]{2,1,0:T(8,128)S(1)}, f32[8,128]{1,0:T(8,128)S(1)}) custom-call(f32[4,64,2048]{2,1,0:T(8,128)} %pot_hbm.3, s32[4,64,2048]{2,1,0:T(8,128)} %reg_hbm.3, f32[4,64,2048]{2,1,0:T(8,128)} %chg_hbm.1, f32[16]{0:T(128)S(1)} %copy-done.1, ...), custom_call_target="tpu_custom_call" | custom-call | flops 20971520 | bytes 4194304 | tf_op jit(solution)/shard_map/pack_rest/pallas_call | solution.py:245
  10.6 0.7 relax.7
  11.4 0.6 collective-permute-start.4
  12.0 0.8 collective-permute-start.7
  12.9 3.8 %collective-permute-start.6 = (f32[32,128]{1,0:T(8,128)S(1)}, f32[32,128]{1,0:T(8,128)S(1)}, u32[]{:S(2)}, u32[]{:S(2)}) collective-permute-start(f32[32,128]{1,0:T(8,128)S(1)} %get-tuple-element.76), channel_id=1, source_target_pairs={{0,8},{8,0},{16,24},{24,16},{32,40},{40,32},{48,56},{56,48},{64,72... | collective-permute-start | bytes 49160 | tf_op jit(solution)/shard_map/ppermute | solution.py:556
  16.7 1.4 %angles.2 = (bf16[4,2048,256]{2,1,0:T(8,128)(2,1)S(1)}, f32[4,64,2048]{2,1,0:T(8,128)S(1)}, f32[8,128]{1,0:T(8,128)S(1)}) custom-call(f32[32,128]{1,0:T(8,128)S(1)} %get-tuple-element.75.after), custom_call_target="tpu_custom_call" | custom-call | flops 8388608 | tf_op jit(solution)/shard_map/angles/pallas_call | solution.py:383
  18.1 0.3 collective-permute-done.6.xe_ref
  18.4 0.8 relax.8
  19.2 3.0 %collective-permute-start.8 = (f32[32,2048]{1,0:T(8,128)S(1)}, f32[32,2048]{1,0:T(8,128)S(1)}, u32[]{:S(2)}, u32[]{:S(2)}) collective-permute-start(f32[32,2048]{1,0:T(8,128)S(1)} %get-tuple-element.80), channel_id=1, source_target_pairs={{1,2},{3,4},{5,6},{9,10},{11,12},{13,14},{17,18},{19,20},{21,22},{... | collective-permute-start | bytes 786440 | tf_op jit(solution)/shard_map/ppermute | solution.py:554
  22.2 0.5 collective-permute-start.9
  22.7 3.8 %collective-permute-start.10 = (f32[32,128]{1,0:T(8,128)S(1)}, f32[32,128]{1,0:T(8,128)S(1)}, u32[]{:S(2)}, u32[]{:S(2)}) collective-permute-start(f32[32,128]{1,0:T(8,128)S(1)} %get-tuple-element.82), channel_id=1, source_target_pairs={{0,8},{8,0},{16,24},{24,16},{32,40},{40,32},{48,56},{56,48},{64,72... | collective-permute-start | bytes 49160 | tf_op jit(solution)/shard_map/ppermute | solution.py:556
  26.5 1.7 %collective-permute-done.10.xe_ref = f32[32,128]{1,0:T(8,128)S(1)} collective-permute-done((f32[32,128]{1,0:T(8,128)S(1)}, f32[32,128]{1,0:T(8,128)S(1)}, u32[]{:S(2)}, u32[]{:S(2)}) %collective-permute-start.10) | collective-permute-done | bytes 16416 | tf_op jit(solution)/shard_map/ppermute | solution.py:556
  28.2 0.8 relax.9
  29.1 1.6 %collective-permute-start.12 = (f32[32,2048]{1,0:T(8,128)S(1)}, f32[32,2048]{1,0:T(8,128)S(1)}, u32[]{:S(2)}, u32[]{:S(2)}) collective-permute-start(f32[32,2048]{1,0:T(8,128)S(1)} %get-tuple-element.85), channel_id=1, source_target_pairs={{1,2},{3,4},{5,6},{9,10},{11,12},{13,14},{17,18},{19,20},{21,22},{... | collective-permute-start | bytes 786440 | tf_op jit(solution)/shard_map/ppermute | solution.py:554
  30.7 0.8 collective-permute-start.14
  31.6 1.4 %angles.3 = (bf16[4,2048,256]{2,1,0:T(8,128)(2,1)S(1)}, f32[4,64,2048]{2,1,0:T(8,128)S(1)}, f32[8,128]{1,0:T(8,128)S(1)}) custom-call(f32[32,128]{1,0:T(8,128)S(1)} %get-tuple-element.86.after), custom_call_target="tpu_custom_call" | custom-call | flops 8388608 | tf_op jit(solution)/shard_map/angles/pallas_call | solution.py:383
  33.0 1.5 %collective-permute-done.14.xe_ref = f32[32,128]{1,0:T(8,128)S(1)} collective-permute-done((f32[32,128]{1,0:T(8,128)S(1)}, f32[32,128]{1,0:T(8,128)S(1)}, u32[]{:S(2)}, u32[]{:S(2)}) %collective-permute-start.14) | collective-permute-done | bytes 16416 | tf_op jit(solution)/shard_map/ppermute | solution.py:556
  34.4 0.5 collective-permute-done.12.ze_ref
  34.9 0.7 relax.10
  35.7 4.0 %collective-permute-start.16 = (f32[32,2048]{1,0:T(8,128)S(1)}, f32[32,2048]{1,0:T(8,128)S(1)}, u32[]{:S(2)}, u32[]{:S(2)}) collective-permute-start(f32[32,2048]{1,0:T(8,128)S(1)} %get-tuple-element.91), channel_id=1, source_target_pairs={{1,2},{3,4},{5,6},{9,10},{11,12},{13,14},{17,18},{19,20},{21,22},{... | collective-permute-start | bytes 786440 | tf_op jit(solution)/shard_map/ppermute | solution.py:554
  39.7 0.5 collective-permute-start.17
  40.2 1.5 %collective-permute-start.18 = (f32[32,128]{1,0:T(8,128)S(1)}, f32[32,128]{1,0:T(8,128)S(1)}, u32[]{:S(2)}, u32[]{:S(2)}) collective-permute-start(f32[32,128]{1,0:T(8,128)S(1)} %get-tuple-element.93), channel_id=1, source_target_pairs={{0,8},{8,0},{16,24},{24,16},{32,40},{40,32},{48,56},{56,48},{64,72... | collective-permute-start | bytes 49160 | tf_op jit(solution)/shard_map/ppermute | solution.py:556
  41.7 2.2 %collective-permute-done.18.xe_ref = f32[32,128]{1,0:T(8,128)S(1)} collective-permute-done((f32[32,128]{1,0:T(8,128)S(1)}, f32[32,128]{1,0:T(8,128)S(1)}, u32[]{:S(2)}, u32[]{:S(2)}) %collective-permute-start.18) | collective-permute-done | bytes 16416 | tf_op jit(solution)/shard_map/ppermute | solution.py:556
  44.0 0.8 relax.11
  44.7 2.7 %collective-permute-start.20 = (f32[32,2048]{1,0:T(8,128)S(1)}, f32[32,2048]{1,0:T(8,128)S(1)}, u32[]{:S(2)}, u32[]{:S(2)}) collective-permute-start(f32[32,2048]{1,0:T(8,128)S(1)} %get-tuple-element.96), channel_id=1, source_target_pairs={{1,2},{3,4},{5,6},{9,10},{11,12},{13,14},{17,18},{19,20},{21,22},{... | collective-permute-start | bytes 786440 | tf_op jit(solution)/shard_map/ppermute | solution.py:554
  47.4 0.5 collective-permute-start.21
  47.9 1.1 %collective-permute-start.22 = (f32[32,128]{1,0:T(8,128)S(1)}, f32[32,128]{1,0:T(8,128)S(1)}, u32[]{:S(2)}, u32[]{:S(2)}) collective-permute-start(f32[32,128]{1,0:T(8,128)S(1)} %get-tuple-element.98), channel_id=1, source_target_pairs={{0,8},{8,0},{16,24},{24,16},{32,40},{40,32},{48,56},{56,48},{64,72... | collective-permute-start | bytes 49160 | tf_op jit(solution)/shard_map/ppermute | solution.py:556
  49.1 2.6 %collective-permute-done.22.xe_ref = f32[32,128]{1,0:T(8,128)S(1)} collective-permute-done((f32[32,128]{1,0:T(8,128)S(1)}, f32[32,128]{1,0:T(8,128)S(1)}, u32[]{:S(2)}, u32[]{:S(2)}) %collective-permute-start.22) | collective-permute-done | bytes 16416 | tf_op jit(solution)/shard_map/ppermute | solution.py:556
  51.7 0.8 relax.12
  52.4 2.9 %collective-permute-start.24 = (f32[32,2048]{1,0:T(8,128)S(1)}, f32[32,2048]{1,0:T(8,128)S(1)}, u32[]{:S(2)}, u32[]{:S(2)}) collective-permute-start(f32[32,2048]{1,0:T(8,128)S(1)} %get-tuple-element.101), channel_id=1, source_target_pairs={{1,2},{3,4},{5,6},{9,10},{11,12},{13,14},{17,18},{19,20},{21,22},{... | collective-permute-start | bytes 786440 | tf_op jit(solution)/shard_map/ppermute | solution.py:554
  55.4 0.5 collective-permute-start.25
  55.9 1.2 %collective-permute-start.26 = (f32[32,128]{1,0:T(8,128)S(1)}, f32[32,128]{1,0:T(8,128)S(1)}, u32[]{:S(2)}, u32[]{:S(2)}) collective-permute-start(f32[32,128]{1,0:T(8,128)S(1)} %get-tuple-element.103), channel_id=1, source_target_pairs={{0,8},{8,0},{16,24},{24,16},{32,40},{40,32},{48,56},{56,48},{64,72... | collective-permute-start | bytes 49160 | tf_op jit(solution)/shard_map/ppermute | solution.py:556
  57.1 2.5 %collective-permute-done.26.xe_ref = f32[32,128]{1,0:T(8,128)S(1)} collective-permute-done((f32[32,128]{1,0:T(8,128)S(1)}, f32[32,128]{1,0:T(8,128)S(1)}, u32[]{:S(2)}, u32[]{:S(2)}) %collective-permute-start.26) | collective-permute-done | bytes 16416 | tf_op jit(solution)/shard_map/ppermute | solution.py:556
  59.6 0.7 relax.13
  60.4 3.3 %collective-permute-start.28 = (f32[32,2048]{1,0:T(8,128)S(1)}, f32[32,2048]{1,0:T(8,128)S(1)}, u32[]{:S(2)}, u32[]{:S(2)}) collective-permute-start(f32[32,2048]{1,0:T(8,128)S(1)} %get-tuple-element.106), channel_id=1, source_target_pairs={{1,2},{3,4},{5,6},{9,10},{11,12},{13,14},{17,18},{19,20},{21,22},{... | collective-permute-start | bytes 786440 | tf_op jit(solution)/shard_map/ppermute | solution.py:554
  63.7 0.5 collective-permute-start.29
  64.2 0.9 %collective-permute-start.30 = (f32[32,128]{1,0:T(8,128)S(1)}, f32[32,128]{1,0:T(8,128)S(1)}, u32[]{:S(2)}, u32[]{:S(2)}) collective-permute-start(f32[32,128]{1,0:T(8,128)S(1)} %get-tuple-element.108), channel_id=1, source_target_pairs={{0,8},{8,0},{16,24},{24,16},{32,40},{40,32},{48,56},{56,48},{64,72... | collective-permute-start | bytes 49160 | tf_op jit(solution)/shard_map/ppermute | solution.py:556
  65.2 2.9 %multipole.1 = (f32[8,256]{1,0:T(8,128)S(1)}, f32[8,128]{1,0:T(8,128)S(1)}) custom-call(f32[4,32,2048]{2,1,0:T(8,128)S(1)} %get-tuple-element.105.field_ref.other_ref, bf16[4,2048,256]{2,1,0:T(8,128)(2,1)S(1)} %get-tuple-element.110.left0, f32[4,64,2048]{2,1,0:T(8,128)S(1)} %get-tuple-element.111.radial0, ...), custom_call_target="tpu_custom_call" | custom-call | flops 26214400 | tf_op jit(solution)/shard_map/multipole/pallas_call | solution.py:460
  68.1 4.3 %relax_last.1 = (f32[4,64,2048]{2,1,0:T(8,128)}, f32[8,256]{1,0:T(8,128)S(1)}) custom-call(f32[4,32,2048]{2,1,0:T(8,128)S(1)} %get-tuple-element.100.other_ref.after.own_ref, f32[4,32,2048]{2,1,0:T(8,128)S(1)} %get-tuple-element.105.field_ref.other_ref, f32[4,32,2048]{2,1,0:T(8,128)S(1)} %get-tuple-element.73.charge_ref, ...), custom_call_target="tpu_custom_call" | custom-call | flops 26214400 | tf_op jit(solution)/shard_map/relax_last/pallas_call | solution.py:511
  72.4 0.1 slice.3
  72.6 0.1 copy.9
  72.8 18.5 %all_to_all.9 = f32[32,1,8]{2,1,0:T(1,128)S(1)} all-to-all(f32[32,1,8]{2,1,0:T(1,128)S(1)} %bitcast.6), channel_id=1, replica_groups=mesh['gx'=32,'gz'=8] {'gx'}, dimensions={0} | all-to-all | bytes 2048 | tf_op jit(solution)/shard_map/all_to_all | solution.py:580
  91.4 0.6 reshape.15
  (40 shorter events, 0.4 us)
Async XLA Ops:
  0.6 0.7 copy-start
  1.3 6.5 %copy-start.1 = (f32[16]{0:T(128)S(1)}, f32[16]{0:T(128)}, u32[]{:S(2)}) copy-start(f32[16]{0:T(128)} %lev_hbm.3) | copy-start | bytes 196
  4.1 6.5 %collective-permute-start = (f32[32,2048]{1,0:T(8,128)S(1)}, f32[32,2048]{1,0:T(8,128)S(1)}, u32[]{:S(2)}, u32[]{:S(2)}) collective-permute-start(f32[32,2048]{1,0:T(8,128)S(1)} %get-tuple-element.68), channel_id=1, source_target_pairs={{1,2},{3,4},{5,6},{9,10},{11,12},{13,14},{17,18},{19,20},{21,22},{... | collective-permute-start | bytes 786440 | tf_op jit(solution)/shard_map/ppermute | solution.py:554
  4.2 6.4 %collective-permute-start.3 = (f32[32,2048]{1,0:T(8,128)S(1)}, f32[32,2048]{1,0:T(8,128)S(1)}, u32[]{:S(2)}, u32[]{:S(2)}) collective-permute-start(f32[32,2048]{1,0:T(8,128)S(1)} %get-tuple-element.70), channel_id=1, source_target_pairs={{0,1},{1,0},{2,3},{3,2},{4,5},{5,4},{6,7},{7,6},{8,9},{9,8},{10,11... | collective-permute-start | bytes 786440 | tf_op jit(solution)/shard_map/ppermute | solution.py:557
  5.9 4.7 %collective-permute-start.2 = (f32[32,128]{1,0:T(8,128)S(1)}, f32[32,128]{1,0:T(8,128)S(1)}, u32[]{:S(2)}, u32[]{:S(2)}) collective-permute-start(f32[32,128]{1,0:T(8,128)S(1)} %get-tuple-element.69), channel_id=1, source_target_pairs={{0,8},{8,0},{16,24},{24,16},{32,40},{40,32},{48,56},{56,48},{64,72... | collective-permute-start | bytes 49160 | tf_op jit(solution)/shard_map/ppermute | solution.py:556
  7.8 2.8 %collective-permute-start.1 = (f32[32,128]{1,0:T(8,128)S(1)}, f32[32,128]{1,0:T(8,128)S(1)}, u32[]{:S(2)}, u32[]{:S(2)}) collective-permute-start(f32[32,128]{1,0:T(8,128)S(1)} %get-tuple-element.64.after), channel_id=1, source_target_pairs={{8,16},{9,17},{10,18},{11,19},{12,20},{13,21},{14,22},{15,23},{24,... | collective-permute-start | bytes 49160 | tf_op jit(solution)/shard_map/ppermute | solution.py:555
  11.4 7.0 %collective-permute-start.4 = (f32[32,2048]{1,0:T(8,128)S(1)}, f32[32,2048]{1,0:T(8,128)S(1)}, u32[]{:S(2)}, u32[]{:S(2)}) collective-permute-start(f32[32,2048]{1,0:T(8,128)S(1)} %get-tuple-element.74), channel_id=1, source_target_pairs={{1,2},{3,4},{5,6},{9,10},{11,12},{13,14},{17,18},{19,20},{21,22},{... | collective-permute-start | bytes 786440 | tf_op jit(solution)/shard_map/ppermute | solution.py:554
  12.0 6.4 %collective-permute-start.7 = (f32[32,2048]{1,0:T(8,128)S(1)}, f32[32,2048]{1,0:T(8,128)S(1)}, u32[]{:S(2)}, u32[]{:S(2)}) collective-permute-start(f32[32,2048]{1,0:T(8,128)S(1)} %get-tuple-element.77), channel_id=1, source_target_pairs={{0,1},{1,0},{2,3},{3,2},{4,5},{5,4},{6,7},{7,6},{8,9},{9,8},{10,11... | collective-permute-start | bytes 786440 | tf_op jit(solution)/shard_map/ppermute | solution.py:557
  12.9 5.5 %collective-permute-start.6 = (f32[32,128]{1,0:T(8,128)S(1)}, f32[32,128]{1,0:T(8,128)S(1)}, u32[]{:S(2)}, u32[]{:S(2)}) collective-permute-start(f32[32,128]{1,0:T(8,128)S(1)} %get-tuple-element.76), channel_id=1, source_target_pairs={{0,8},{8,0},{16,24},{24,16},{32,40},{40,32},{48,56},{56,48},{64,72... | collective-permute-start | bytes 49160 | tf_op jit(solution)/shard_map/ppermute | solution.py:556
  16.7 1.7 %collective-permute-start.5 = (f32[32,128]{1,0:T(8,128)S(1)}, f32[32,128]{1,0:T(8,128)S(1)}, u32[]{:S(2)}, u32[]{:S(2)}) collective-permute-start(f32[32,128]{1,0:T(8,128)S(1)} %get-tuple-element.75.after), channel_id=1, source_target_pairs={{8,16},{9,17},{10,18},{11,19},{12,20},{13,21},{14,22},{15,23},{24,... | collective-permute-start | bytes 49160 | tf_op jit(solution)/shard_map/ppermute | solution.py:555
  19.2 9.0 %collective-permute-start.8 = (f32[32,2048]{1,0:T(8,128)S(1)}, f32[32,2048]{1,0:T(8,128)S(1)}, u32[]{:S(2)}, u32[]{:S(2)}) collective-permute-start(f32[32,2048]{1,0:T(8,128)S(1)} %get-tuple-element.80), channel_id=1, source_target_pairs={{1,2},{3,4},{5,6},{9,10},{11,12},{13,14},{17,18},{19,20},{21,22},{... | collective-permute-start | bytes 786440 | tf_op jit(solution)/shard_map/ppermute | solution.py:554
  22.2 6.0 %collective-permute-start.11 = (f32[32,2048]{1,0:T(8,128)S(1)}, f32[32,2048]{1,0:T(8,128)S(1)}, u32[]{:S(2)}, u32[]{:S(2)}) collective-permute-start(f32[32,2048]{1,0:T(8,128)S(1)} %get-tuple-element.83), channel_id=1, source_target_pairs={{0,1},{1,0},{2,3},{3,2},{4,5},{5,4},{6,7},{7,6},{8,9},{9,8},{10,11... | collective-permute-start | bytes 786440 | tf_op jit(solution)/shard_map/ppermute | solution.py:557
  22.2 4.3 %collective-permute-start.9 = (f32[32,128]{1,0:T(8,128)S(1)}, f32[32,128]{1,0:T(8,128)S(1)}, u32[]{:S(2)}, u32[]{:S(2)}) collective-permute-start(f32[32,128]{1,0:T(8,128)S(1)} %get-tuple-element.81), channel_id=1, source_target_pairs={{8,16},{9,17},{10,18},{11,19},{12,20},{13,21},{14,22},{15,23},{24,... | collective-permute-start | bytes 49160 | tf_op jit(solution)/shard_map/ppermute | solution.py:555
  22.7 5.5 %collective-permute-start.10 = (f32[32,128]{1,0:T(8,128)S(1)}, f32[32,128]{1,0:T(8,128)S(1)}, u32[]{:S(2)}, u32[]{:S(2)}) collective-permute-start(f32[32,128]{1,0:T(8,128)S(1)} %get-tuple-element.82), channel_id=1, source_target_pairs={{0,8},{8,0},{16,24},{24,16},{32,40},{40,32},{48,56},{56,48},{64,72... | collective-permute-start | bytes 49160 | tf_op jit(solution)/shard_map/ppermute | solution.py:556
  29.1 5.9 %collective-permute-start.12 = (f32[32,2048]{1,0:T(8,128)S(1)}, f32[32,2048]{1,0:T(8,128)S(1)}, u32[]{:S(2)}, u32[]{:S(2)}) collective-permute-start(f32[32,2048]{1,0:T(8,128)S(1)} %get-tuple-element.85), channel_id=1, source_target_pairs={{1,2},{3,4},{5,6},{9,10},{11,12},{13,14},{17,18},{19,20},{21,22},{... | collective-permute-start | bytes 786440 | tf_op jit(solution)/shard_map/ppermute | solution.py:554
  30.7 4.3 %collective-permute-start.15 = (f32[32,2048]{1,0:T(8,128)S(1)}, f32[32,2048]{1,0:T(8,128)S(1)}, u32[]{:S(2)}, u32[]{:S(2)}) collective-permute-start(f32[32,2048]{1,0:T(8,128)S(1)} %get-tuple-element.88), channel_id=1, source_target_pairs={{0,1},{1,0},{2,3},{3,2},{4,5},{5,4},{6,7},{7,6},{8,9},{9,8},{10,11... | collective-permute-start | bytes 786440 | tf_op jit(solution)/shard_map/ppermute | solution.py:557
  30.7 3.7 %collective-permute-start.14 = (f32[32,128]{1,0:T(8,128)S(1)}, f32[32,128]{1,0:T(8,128)S(1)}, u32[]{:S(2)}, u32[]{:S(2)}) collective-permute-start(f32[32,128]{1,0:T(8,128)S(1)} %get-tuple-element.87), channel_id=1, source_target_pairs={{0,8},{8,0},{16,24},{24,16},{32,40},{40,32},{48,56},{56,48},{64,72... | collective-permute-start | bytes 49160 | tf_op jit(solution)/shard_map/ppermute | solution.py:556
  31.5 2.9 %collective-permute-start.13 = (f32[32,128]{1,0:T(8,128)S(1)}, f32[32,128]{1,0:T(8,128)S(1)}, u32[]{:S(2)}, u32[]{:S(2)}) collective-permute-start(f32[32,128]{1,0:T(8,128)S(1)} %get-tuple-element.86.after), channel_id=1, source_target_pairs={{8,16},{9,17},{10,18},{11,19},{12,20},{13,21},{14,22},{15,23},{24,... | collective-permute-start | bytes 49160 | tf_op jit(solution)/shard_map/ppermute | solution.py:555
  35.7 8.3 %collective-permute-start.16 = (f32[32,2048]{1,0:T(8,128)S(1)}, f32[32,2048]{1,0:T(8,128)S(1)}, u32[]{:S(2)}, u32[]{:S(2)}) collective-permute-start(f32[32,2048]{1,0:T(8,128)S(1)} %get-tuple-element.91), channel_id=1, source_target_pairs={{1,2},{3,4},{5,6},{9,10},{11,12},{13,14},{17,18},{19,20},{21,22},{... | collective-permute-start | bytes 786440 | tf_op jit(solution)/shard_map/ppermute | solution.py:554
  39.7 4.3 %collective-permute-start.19 = (f32[32,2048]{1,0:T(8,128)S(1)}, f32[32,2048]{1,0:T(8,128)S(1)}, u32[]{:S(2)}, u32[]{:S(2)}) collective-permute-start(f32[32,2048]{1,0:T(8,128)S(1)} %get-tuple-element.94), channel_id=1, source_target_pairs={{0,1},{1,0},{2,3},{3,2},{4,5},{5,4},{6,7},{7,6},{8,9},{9,8},{10,11... | collective-permute-start | bytes 786440 | tf_op jit(solution)/shard_map/ppermute | solution.py:557
  39.7 2.0 %collective-permute-start.17 = (f32[32,128]{1,0:T(8,128)S(1)}, f32[32,128]{1,0:T(8,128)S(1)}, u32[]{:S(2)}, u32[]{:S(2)}) collective-permute-start(f32[32,128]{1,0:T(8,128)S(1)} %get-tuple-element.92), channel_id=1, source_target_pairs={{8,16},{9,17},{10,18},{11,19},{12,20},{13,21},{14,22},{15,23},{24,... | collective-permute-start | bytes 49160 | tf_op jit(solution)/shard_map/ppermute | solution.py:555
  40.2 3.7 %collective-permute-start.18 = (f32[32,128]{1,0:T(8,128)S(1)}, f32[32,128]{1,0:T(8,128)S(1)}, u32[]{:S(2)}, u32[]{:S(2)}) collective-permute-start(f32[32,128]{1,0:T(8,128)S(1)} %get-tuple-element.93), channel_id=1, source_target_pairs={{0,8},{8,0},{16,24},{24,16},{32,40},{40,32},{48,56},{56,48},{64,72... | collective-permute-start | bytes 49160 | tf_op jit(solution)/shard_map/ppermute | solution.py:556
  44.7 6.9 %collective-permute-start.20 = (f32[32,2048]{1,0:T(8,128)S(1)}, f32[32,2048]{1,0:T(8,128)S(1)}, u32[]{:S(2)}, u32[]{:S(2)}) collective-permute-start(f32[32,2048]{1,0:T(8,128)S(1)} %get-tuple-element.96), channel_id=1, source_target_pairs={{1,2},{3,4},{5,6},{9,10},{11,12},{13,14},{17,18},{19,20},{21,22},{... | collective-permute-start | bytes 786440 | tf_op jit(solution)/shard_map/ppermute | solution.py:554
  47.4 4.3 %collective-permute-start.23 = (f32[32,2048]{1,0:T(8,128)S(1)}, f32[32,2048]{1,0:T(8,128)S(1)}, u32[]{:S(2)}, u32[]{:S(2)}) collective-permute-start(f32[32,2048]{1,0:T(8,128)S(1)} %get-tuple-element.99), channel_id=1, source_target_pairs={{0,1},{1,0},{2,3},{3,2},{4,5},{5,4},{6,7},{7,6},{8,9},{9,8},{10,11... | collective-permute-start | bytes 786440 | tf_op jit(solution)/shard_map/ppermute | solution.py:557
  47.4 1.7 %collective-permute-start.21 = (f32[32,128]{1,0:T(8,128)S(1)}, f32[32,128]{1,0:T(8,128)S(1)}, u32[]{:S(2)}, u32[]{:S(2)}) collective-permute-start(f32[32,128]{1,0:T(8,128)S(1)} %get-tuple-element.97), channel_id=1, source_target_pairs={{8,16},{9,17},{10,18},{11,19},{12,20},{13,21},{14,22},{15,23},{24,... | collective-permute-start | bytes 49160 | tf_op jit(solution)/shard_map/ppermute | solution.py:555
  47.9 3.7 %collective-permute-start.22 = (f32[32,128]{1,0:T(8,128)S(1)}, f32[32,128]{1,0:T(8,128)S(1)}, u32[]{:S(2)}, u32[]{:S(2)}) collective-permute-start(f32[32,128]{1,0:T(8,128)S(1)} %get-tuple-element.98), channel_id=1, source_target_pairs={{0,8},{8,0},{16,24},{24,16},{32,40},{40,32},{48,56},{56,48},{64,72... | collective-permute-start | bytes 49160 | tf_op jit(solution)/shard_map/ppermute | solution.py:556
  52.4 7.2 %collective-permute-start.24 = (f32[32,2048]{1,0:T(8,128)S(1)}, f32[32,2048]{1,0:T(8,128)S(1)}, u32[]{:S(2)}, u32[]{:S(2)}) collective-permute-start(f32[32,2048]{1,0:T(8,128)S(1)} %get-tuple-element.101), channel_id=1, source_target_pairs={{1,2},{3,4},{5,6},{9,10},{11,12},{13,14},{17,18},{19,20},{21,22},{... | collective-permute-start | bytes 786440 | tf_op jit(solution)/shard_map/ppermute | solution.py:554
  55.4 4.3 %collective-permute-start.27 = (f32[32,2048]{1,0:T(8,128)S(1)}, f32[32,2048]{1,0:T(8,128)S(1)}, u32[]{:S(2)}, u32[]{:S(2)}) collective-permute-start(f32[32,2048]{1,0:T(8,128)S(1)} %get-tuple-element.104), channel_id=1, source_target_pairs={{0,1},{1,0},{2,3},{3,2},{4,5},{5,4},{6,7},{7,6},{8,9},{9,8},{10,11... | collective-permute-start | bytes 786440 | tf_op jit(solution)/shard_map/ppermute | solution.py:557
  55.4 1.7 %collective-permute-start.25 = (f32[32,128]{1,0:T(8,128)S(1)}, f32[32,128]{1,0:T(8,128)S(1)}, u32[]{:S(2)}, u32[]{:S(2)}) collective-permute-start(f32[32,128]{1,0:T(8,128)S(1)} %get-tuple-element.102), channel_id=1, source_target_pairs={{8,16},{9,17},{10,18},{11,19},{12,20},{13,21},{14,22},{15,23},{24,... | collective-permute-start | bytes 49160 | tf_op jit(solution)/shard_map/ppermute | solution.py:555
  55.9 3.7 %collective-permute-start.26 = (f32[32,128]{1,0:T(8,128)S(1)}, f32[32,128]{1,0:T(8,128)S(1)}, u32[]{:S(2)}, u32[]{:S(2)}) collective-permute-start(f32[32,128]{1,0:T(8,128)S(1)} %get-tuple-element.103), channel_id=1, source_target_pairs={{0,8},{8,0},{16,24},{24,16},{32,40},{40,32},{48,56},{56,48},{64,72... | collective-permute-start | bytes 49160 | tf_op jit(solution)/shard_map/ppermute | solution.py:556
  60.4 7.7 %collective-permute-start.28 = (f32[32,2048]{1,0:T(8,128)S(1)}, f32[32,2048]{1,0:T(8,128)S(1)}, u32[]{:S(2)}, u32[]{:S(2)}) collective-permute-start(f32[32,2048]{1,0:T(8,128)S(1)} %get-tuple-element.106), channel_id=1, source_target_pairs={{1,2},{3,4},{5,6},{9,10},{11,12},{13,14},{17,18},{19,20},{21,22},{... | collective-permute-start | bytes 786440 | tf_op jit(solution)/shard_map/ppermute | solution.py:554
  63.7 4.4 %collective-permute-start.31 = (f32[32,2048]{1,0:T(8,128)S(1)}, f32[32,2048]{1,0:T(8,128)S(1)}, u32[]{:S(2)}, u32[]{:S(2)}) collective-permute-start(f32[32,2048]{1,0:T(8,128)S(1)} %get-tuple-element.109), channel_id=1, source_target_pairs={{0,1},{1,0},{2,3},{3,2},{4,5},{5,4},{6,7},{7,6},{8,9},{9,8},{10,11... | collective-permute-start | bytes 786440 | tf_op jit(solution)/shard_map/ppermute | solution.py:557
  63.7 4.4 %collective-permute-start.29 = (f32[32,128]{1,0:T(8,128)S(1)}, f32[32,128]{1,0:T(8,128)S(1)}, u32[]{:S(2)}, u32[]{:S(2)}) collective-permute-start(f32[32,128]{1,0:T(8,128)S(1)} %get-tuple-element.107), channel_id=1, source_target_pairs={{8,16},{9,17},{10,18},{11,19},{12,20},{13,21},{14,22},{15,23},{24,... | collective-permute-start | bytes 49160 | tf_op jit(solution)/shard_map/ppermute | solution.py:555
  64.2 3.9 %collective-permute-start.30 = (f32[32,128]{1,0:T(8,128)S(1)}, f32[32,128]{1,0:T(8,128)S(1)}, u32[]{:S(2)}, u32[]{:S(2)}) collective-permute-start(f32[32,128]{1,0:T(8,128)S(1)} %get-tuple-element.108), channel_id=1, source_target_pairs={{0,8},{8,0},{16,24},{24,16},{32,40},{40,32},{48,56},{56,48},{64,72... | collective-permute-start | bytes 49160 | tf_op jit(solution)/shard_map/ppermute | solution.py:556
